TPU v7x, 32 devices: a whole 2x2x4 slice. The times are simulated.
32 devices in a mesh: ctx: 4 (over z), lag: 4 (over x, core), chan: 2 (over y).
Axes of the slice: x: 2, y: 2, z: 4, core: 2. Of those that a mesh axis runs over, the one named last changes fastest.
Arguments:
- values: bfloat16 [512, 8192], P('ctx', 'chan'), may hold values from -6 to 6
- gate: bfloat16 [512, 8192], P('ctx', ('chan', 'lag')), may hold values from -6 to 6
- bias: float32 [8192], P('chan'), may hold values from -6 to 6
- filter_taps: bfloat16 [512, 8192], P('ctx', 'chan'), may hold values from -2 to 2
Outputs:
- mixed: bfloat16 [512, 8192], P('ctx', ('chan', 'lag'))
All inputs are finite; a program needn't handle non-finite values.
Results may differ from a plain program's by a relative error of at most 0.006.
Values may be sent and summed in bfloat16 or wider, within the bound.
No kernel may reach another device: no remote copies, remote signals or barrier semaphores. Data moves between devices by JAX's collectives and lax.ppermute only.
A program may use at most 64 MiB of HBM per device.

v0:
```python
import math

import jax
import jax.numpy as jnp
from jax import lax
from jax.sharding import PartitionSpec as P


def split_table(table):
    upper = table.astype(jnp.bfloat16)
    widened = lax.optimization_barrier(upper).astype(jnp.float32)
    lower = (table - widened).astype(jnp.bfloat16)
    return (upper, lower)


def dft_tables(length, first, count):
    frequency = jnp.arange(length // 2 + 1, dtype=jnp.int32)[:, None]
    item_step_index = first + jnp.arange(count, dtype=jnp.int32)[None, :]
    phase_turns = frequency * item_step_index % length
    phase_angles = phase_turns.astype(jnp.float32) * (2.0 * math.pi / length)
    return (split_table(jnp.cos(phase_angles)), split_table(-jnp.sin(phase_angles)))


def inverse_tables(length, rows):
    row_index = jnp.arange(rows, dtype=jnp.int32)[:, None]
    frequency = jnp.arange(length // 2 + 1, dtype=jnp.int32)[None, :]
    phase_turns = frequency * row_index % length
    phase_angles = phase_turns.astype(jnp.float32) * (2.0 * math.pi / length)
    weights = jnp.where((frequency == 0) | (frequency == length // 2), 1.0, 2.0).astype(jnp.float32)
    return (weights * jnp.cos(phase_angles) / length, -weights * jnp.sin(phase_angles) / length)


def transform(tables, operand):
    cos_parts, sin_parts = tables
    real_part = jnp.einsum(
        "fm,...mc->...fc", cos_parts[0], operand, preferred_element_type=jnp.float32
    )
    real_part = real_part + jnp.einsum(
        "fm,...mc->...fc", cos_parts[1], operand, preferred_element_type=jnp.float32
    )
    imag_part = jnp.einsum(
        "fm,...mc->...fc", sin_parts[0], operand, preferred_element_type=jnp.float32
    )
    imag_part = imag_part + jnp.einsum(
        "fm,...mc->...fc", sin_parts[1], operand, preferred_element_type=jnp.float32
    )
    return (real_part, imag_part)


def spectrum_pair(low_tables, high_tables, current, previous):
    first_re, first_im = transform(low_tables, current)
    second_re, second_im = transform(high_tables, previous)
    return (first_re + second_re, first_im + second_im)


def inverse(back_cos, back_sin, total_re, total_im):
    result = jnp.einsum(
        "rf,...fc->...rc",
        back_cos,
        total_re,
        precision=lax.Precision.HIGHEST,
        preferred_element_type=jnp.float32,
    )
    return result + jnp.einsum(
        "rf,...fc->...rc",
        back_sin,
        total_im,
        precision=lax.Precision.HIGHEST,
        preferred_element_type=jnp.float32,
    )


def body(values, gate, bias, filter_taps):
    tok_rows = values.shape[0]
    length = 2 * tok_rows
    lag_count = lax.axis_size("lag")
    lag_index = lax.axis_index("lag")
    low_tables = dft_tables(length, 0, tok_rows)
    high_tables = dft_tables(length, tok_rows, tok_rows)
    back_cos, back_sin = inverse_tables(length, tok_rows)
    share_width = values.shape[1] // lag_count
    value_share = lax.dynamic_slice_in_dim(values, lag_index * share_width, share_width, 1)
    taps_share = lax.dynamic_slice_in_dim(filter_taps, lag_index * share_width, share_width, 1)
    cols_values, cols_taps = (
        lax.all_to_all(value_share, "ctx", split_axis=1, concat_axis=0, tiled=True),
        lax.all_to_all(taps_share, "ctx", split_axis=1, concat_axis=0, tiled=True),
    )
    block_count = lax.axis_size("ctx")
    narrow = cols_values.shape[1]
    value_blocks = cols_values.reshape(block_count, tok_rows, narrow)
    taps_blocks = cols_taps.reshape(block_count, tok_rows, narrow)
    earlier = jnp.concatenate([jnp.zeros_like(taps_blocks[:1]), taps_blocks[:-1]], axis=0)
    kernel_real_entry, filt_im = spectrum_pair(low_tables, high_tables, taps_blocks, earlier)
    val_re, val_im = transform(low_tables, value_blocks)
    padded_re = jnp.concatenate([jnp.zeros_like(val_re), val_re], axis=0)
    padded_im = jnp.concatenate([jnp.zeros_like(val_im), val_im], axis=0)

    def add_lag(lag_step, carry):
        acc_re, acc_im = carry
        start = (block_count - lag_step).astype(jnp.int32)
        moved_re = lax.dynamic_slice_in_dim(padded_re, start, block_count, 0)
        moved_im = lax.dynamic_slice_in_dim(padded_im, start, block_count, 0)
        coef_re = lax.dynamic_index_in_dim(kernel_real_entry, lag_step, 0, keepdims=True)
        coef_im = lax.dynamic_index_in_dim(filt_im, lag_step, 0, keepdims=True)
        acc_re = acc_re + coef_re * moved_re - coef_im * moved_im
        acc_im = acc_im + coef_re * moved_im + coef_im * moved_re
        return (acc_re, acc_im)

    empty = jnp.zeros(val_re.shape, jnp.float32)
    total_re, total_im = lax.fori_loop(0, block_count, add_lag, (empty, empty))
    convolved = inverse(back_cos, back_sin, total_re, total_im).reshape(
        block_count * tok_rows, narrow
    )
    ctx_index = lax.axis_index("ctx")
    own_bias = lax.dynamic_slice_in_dim(
        bias, lag_index * share_width + ctx_index * narrow, narrow, 0
    )
    before_gate = convolved + own_bias[None, :] * cols_values.astype(jnp.float32)
    returned = lax.all_to_all(before_gate, "ctx", split_axis=0, concat_axis=1, tiled=True)
    mixed = gate.astype(jnp.float32) * returned
    return mixed.astype(jnp.bfloat16)


def solution(mesh):
    return jax.shard_map(
        body,
        mesh=mesh,
        in_specs=(P("ctx", "chan"), P("ctx", ("chan", "lag")), P("chan"), P("ctx", "chan")),
        out_specs=P("ctx", ("chan", "lag")),
        check_vma=False,
    )
```

profile of v0, /device:TPU:0, one launch (start us, length us, event | category | flops | bytes accessed | tf_op | source)
XLA Modules:
  0.0 63.4 jit_solution(15772436999873901869)
XLA Ops:
  0.0 1.1 %constant_dynamic-slice_fusion = (bf16[128,1024]{1,0:T(8,128)(2,1)S(1)}, bf16[128,1024]{1,0:T(8,128)(2,1)S(1)}) fusion(bf16[128,4096]{1,0:T(8,128)(2,1)} %param.6, s32[]{:T(128)S(6)} %select_n.85, bf16[128,4096]{1,0:T(8,128)(2,1)} %param.9), kind=kLoop, calls=%fused_computation.115 | loop fusion | bytes 1048580 | tf_op jit(solution)/shard_map/dynamic_slice | solution.py:82
  1.1 0.2 copy.18
  1.2 0.9 %copy.9 = bf16[128,4,256]{2,0,1:T(8,128)(2,1)} copy(bf16[128,4,256]{0,2,1:T(8,128)(2,1)S(1)} %bitcast.87) | data formatting | bytes 524288 | tf_op jit(solution)/shard_map/all_to_all | solution.py:86
  2.1 6.3 %all-to-all-start = ((bf16[128,4,256]{2,0,1:T(8,128)(2,1)}), bf16[128,4,256]{2,0,1:T(8,128)(2,1)S(1)}, u32[]{:S(2)}, u32[]{:S(2)}) async-start(bf16[128,4,256]{2,0,1:T(8,128)(2,1)} %copy.9), calls=%async_computation | async-start | bytes 524288 | tf_op jit(solution)/shard_map/all_to_all | solution.py:86
  8.4 0.3 fusion.51
  8.7 0.3 fusion.50
  9.0 0.3 fusion.75
  9.3 0.2 copy.19
  9.5 0.9 %copy.11 = bf16[128,4,256]{2,0,1:T(8,128)(2,1)} copy(bf16[128,4,256]{0,2,1:T(8,128)(2,1)S(1)} %bitcast.88) | data formatting | bytes 524288 | tf_op jit(solution)/shard_map/all_to_all | solution.py:85
  10.4 0.8 %dynamic_slice.52 = f32[256]{0:T(256)S(1)} dynamic-slice(f32[4096]{0:T(1024)} %param.8, s32[]{:T(128)S(6)} %select_n.90), dynamic_slice_sizes={256} | dynamic-slice | bytes 2052 | tf_op jit(solution)/shard_map/dynamic_slice | solution.py:115
  11.1 6.2 %all-to-all-done = bf16[128,4,256]{2,0,1:T(8,128)(2,1)S(1)} async-done(((bf16[128,4,256]{2,0,1:T(8,128)(2,1)}), bf16[128,4,256]{2,0,1:T(8,128)(2,1)S(1)}, u32[]{:S(2)}, u32[]{:S(2)}) %all-to-all-start) | async-done | bytes 262176 | tf_op jit(solution)/shard_map/all_to_all | solution.py:86
  17.3 3.4 %all-to-all-start.1 = ((bf16[128,4,256]{2,0,1:T(8,128)(2,1)}), bf16[128,4,256]{2,0,1:T(8,128)(2,1)S(1)}, u32[]{:S(2)}, u32[]{:S(2)}) async-start(bf16[128,4,256]{2,0,1:T(8,128)(2,1)} %copy.11), calls=%async_computation.1 | async-start | bytes 524288 | tf_op jit(solution)/shard_map/all_to_all | solution.py:85
  20.7 1.3 %fusion.17 = f32[4,256,129]{1,2,0:T(8,128)} fusion(bf16[4,128,256]{2,1,0:T(8,128)(2,1)S(1)} %bitcast.82, s32[128]{0:T(128)S(1)} %iota_add_fusion), kind=kOutput, calls=%fused_computation.29 | convolution fusion | flops 25626624 | bytes 725504 | tf_op jit(solution)/shard_map/fm,...mc->...fc/dot_general | solution.py:41
  22.0 0.4 fusion.20
  22.5 5.3 %all-to-all-done.1 = bf16[128,4,256]{2,0,1:T(8,128)(2,1)S(1)} async-done(((bf16[128,4,256]{2,0,1:T(8,128)(2,1)}), bf16[128,4,256]{2,0,1:T(8,128)(2,1)S(1)}, u32[]{:S(2)}, u32[]{:S(2)}) %all-to-all-start.1) | async-done | bytes 262176 | tf_op jit(solution)/shard_map/all_to_all | solution.py:85
  27.7 0.4 fusion.15
  28.2 0.4 fusion.3
  28.6 0.1 concatenate.10
  28.7 0.4 fusion.12
  29.2 0.4 fusion.2
  29.6 0.0 copy-start
  29.6 1.1 %concatenate.11 = f32[8,129,256]{2,1,0:T(8,128)} pad(f32[4,129,256]{2,1,0:T(8,128)S(1)} %fusion.2, f32[]{:T(128)} %constant.97.clone.1), padding=4_0x0_0x0_0 | pad | bytes 1585156 | tf_op jit(solution)/shard_map/concatenate | solution.py:96
  30.7 0.1 copy-done
  30.8 0.5 convolution_add_fusion
  31.3 0.4 convolution_add_fusion.1
  31.7 0.4 fusion.60
  32.2 0.4 fusion.64
  32.6 0.4 fusion.7
  33.0 1.3 %fusion.5 = f32[4,129,256]{2,1,0:T(8,128)} fusion(f32[4,256,129]{1,2,0:T(8,128)S(1)} %convolution_add_fusion.1, f32[4,256,129]{1,2,0:T(8,128)S(1)} %fusion.64, bf16[129,128]{1,0:T(8,128)(2,1)S(1)} %fusion.75, bf16[128,4,256]{2,0,1:T(8,128)(2,1)S(1)} %all-to-all-done), kind=kOutput, calls=%fused_computation.15 | convolution fusion | flops 34361472 | bytes 1880320 | tf_op jit(solution)/shard_map/fm,...mc->...fc/dot_general | solution.py:38
  34.3 10.1 %while.18 = (s32[]{:T(128)}, f32[4,129,256]{2,1,0:T(8,128)S(1)}, f32[4,129,256]{2,1,0:T(8,128)S(1)}, f32[4,129,256]{2,1,0:T(8,128)}, f32[8,129,256]{2,1,0:T(8,12...) while((s32[]{:T(128)}, f32[4,129,256]{2,1,0:T(8,128)S(1)}, ...), condition=%wide.region_1.2_spmd.clone, body=%wide.region_0.1_spmd.clone.sunk | while | flops 1320967 | bytes 3963053 | solution.py:110
  34.3 0.9 %dynamic-slice_bitcast_fusion.3 = (f32[129,256]{1,0:T(8,128)S(1)}, f32[129,256]{1,0:T(8,128)S(1)}) fusion(f32[4,129,256]{2,1,0:T(8,128)S(1)} %get-tuple-element.308, s32[]{:T(128)} %get-tuple-element.292, f32[4,129,256]{2,1,0:T(8,128)} %get-tuple-element.306), kind=kLoop, calls=%fused_computation.4.clone.1 | loop fusion | bytes 528388 | tf_op jit(solution)/shard_map/while/body/eval_jaxpr/mul | solution.py:105
  35.3 1.6 %fusion.154 = (f32[4,129,256]{2,1,0:T(8,128)S(1)}, f32[4,129,256]{2,1,0:T(8,128)S(1)}) fusion(f32[4,129,256]{2,1,0:T(8,128)S(1)} %get-tuple-element.294, f32[8,129,256]{2,1,0:T(8,128)} %get-tuple-element.309, s32[]{:T(128)S(6)} %select_n.161, f32[8,129,256]{2,1,0:T(8,128)S(1)} %get-tuple-element.307, f32[129,256]{1,0:T(8,128)S(1)} %get-tuple-element.277, ...), kind=kLoop, calls=%fused_computation.1.clone.1 | loop fusion | flops 1320960 | bytes 3434501 | tf_op jit(solution)/shard_map/while/body/eval_jaxpr/add | solution.py:106
  36.9 0.9 %dynamic-slice_bitcast_fusion.3 = (f32[129,256]{1,0:T(8,128)S(1)}, f32[129,256]{1,0:T(8,128)S(1)}) fusion(f32[4,129,256]{2,1,0:T(8,128)S(1)} %get-tuple-element.308, s32[]{:T(128)} %get-tuple-element.292, f32[4,129,256]{2,1,0:T(8,128)} %get-tuple-element.306), kind=kLoop, calls=%fused_computation.4.clone.1 | loop fusion | bytes 528388 | tf_op jit(solution)/shard_map/while/body/eval_jaxpr/mul | solution.py:105
  37.8 1.6 %fusion.154 = (f32[4,129,256]{2,1,0:T(8,128)S(1)}, f32[4,129,256]{2,1,0:T(8,128)S(1)}) fusion(f32[4,129,256]{2,1,0:T(8,128)S(1)} %get-tuple-element.294, f32[8,129,256]{2,1,0:T(8,128)} %get-tuple-element.309, s32[]{:T(128)S(6)} %select_n.161, f32[8,129,256]{2,1,0:T(8,128)S(1)} %get-tuple-element.307, f32[129,256]{1,0:T(8,128)S(1)} %get-tuple-element.277, ...), kind=kLoop, calls=%fused_computation.1.clone.1 | loop fusion | flops 1320960 | bytes 3434501 | tf_op jit(solution)/shard_map/while/body/eval_jaxpr/add | solution.py:106
  39.4 0.9 %dynamic-slice_bitcast_fusion.3 = (f32[129,256]{1,0:T(8,128)S(1)}, f32[129,256]{1,0:T(8,128)S(1)}) fusion(f32[4,129,256]{2,1,0:T(8,128)S(1)} %get-tuple-element.308, s32[]{:T(128)} %get-tuple-element.292, f32[4,129,256]{2,1,0:T(8,128)} %get-tuple-element.306), kind=kLoop, calls=%fused_computation.4.clone.1 | loop fusion | bytes 528388 | tf_op jit(solution)/shard_map/while/body/eval_jaxpr/mul | solution.py:105
  40.3 1.6 %fusion.154 = (f32[4,129,256]{2,1,0:T(8,128)S(1)}, f32[4,129,256]{2,1,0:T(8,128)S(1)}) fusion(f32[4,129,256]{2,1,0:T(8,128)S(1)} %get-tuple-element.294, f32[8,129,256]{2,1,0:T(8,128)} %get-tuple-element.309, s32[]{:T(128)S(6)} %select_n.161, f32[8,129,256]{2,1,0:T(8,128)S(1)} %get-tuple-element.307, f32[129,256]{1,0:T(8,128)S(1)} %get-tuple-element.277, ...), kind=kLoop, calls=%fused_computation.1.clone.1 | loop fusion | flops 1320960 | bytes 3434501 | tf_op jit(solution)/shard_map/while/body/eval_jaxpr/add | solution.py:106
  41.9 0.9 %dynamic-slice_bitcast_fusion.3 = (f32[129,256]{1,0:T(8,128)S(1)}, f32[129,256]{1,0:T(8,128)S(1)}) fusion(f32[4,129,256]{2,1,0:T(8,128)S(1)} %get-tuple-element.308, s32[]{:T(128)} %get-tuple-element.292, f32[4,129,256]{2,1,0:T(8,128)} %get-tuple-element.306), kind=kLoop, calls=%fused_computation.4.clone.1 | loop fusion | bytes 528388 | tf_op jit(solution)/shard_map/while/body/eval_jaxpr/mul | solution.py:105
  42.9 1.6 %fusion.154 = (f32[4,129,256]{2,1,0:T(8,128)S(1)}, f32[4,129,256]{2,1,0:T(8,128)S(1)}) fusion(f32[4,129,256]{2,1,0:T(8,128)S(1)} %get-tuple-element.294, f32[8,129,256]{2,1,0:T(8,128)} %get-tuple-element.309, s32[]{:T(128)S(6)} %select_n.161, f32[8,129,256]{2,1,0:T(8,128)S(1)} %get-tuple-element.307, f32[129,256]{1,0:T(8,128)S(1)} %get-tuple-element.277, ...), kind=kLoop, calls=%fused_computation.1.clone.1 | loop fusion | flops 1320960 | bytes 3434501 | tf_op jit(solution)/shard_map/while/body/eval_jaxpr/add | solution.py:106
  44.5 0.9 %fusion.33 = f32[4,256,128]{1,2,0:T(8,128)S(1)} fusion(f32[4,129,256]{2,1,0:T(8,128)S(1)} %get-tuple-element.182, f32[129]{0:T(256)S(1)} %or_select_fusion), kind=kOutput, calls=%fused_computation.54 | convolution fusion | flops 203163648 | bytes 1053188 | tf_op jit(solution)/shard_map/rf,...fc->...rc/dot_general | solution.py:57
  45.3 0.0 copy-start.1
  45.4 1.7 %fusion.9 = f32[4,128,256]{2,1,0:T(8,128)} fusion(f32[4,256,128]{1,2,0:T(8,128)S(1)} %fusion.33, f32[4,129,256]{2,1,0:T(8,128)S(1)} %get-tuple-element.183, bf16[128,4,256]{2,0,1:T(8,128)(2,1)S(1)} %all-to-all-done.1, f32[256]{0:T(256)S(1)} %dynamic_slice.52, f32[129]{0:T(256)S(1)} %fusion.102), kind=kOutput, calls=%fused_computation.20 | convolution fusion | flops 203687936 | bytes 1840644 | tf_op jit(solution)/shard_map/rf,...fc->...rc/dot_general | solution.py:64
  47.1 3.5 %all-to-all-start.2 = ((f32[4,128,256]{2,1,0:T(8,128)}), f32[4,128,256]{2,1,0:T(8,128)S(1)}, u32[]{:S(2)}, u32[]{:S(2)}) async-start(f32[4,128,256]{2,1,0:T(8,128)} %fusion.9), calls=%async_computation.2 | async-start | bytes 1048576 | tf_op jit(solution)/shard_map/all_to_all | solution.py:119
  50.6 0.0 copy-done.1
  50.6 0.2 copy.7
  50.8 11.5 %all-to-all-done.2 = f32[4,128,256]{2,1,0:T(8,128)S(1)} async-done(((f32[4,128,256]{2,1,0:T(8,128)}), f32[4,128,256]{2,1,0:T(8,128)S(1)}, u32[]{:S(2)}, u32[]{:S(2)}) %all-to-all-start.2) | async-done | bytes 524320 | tf_op jit(solution)/shard_map/all_to_all | solution.py:119
  62.3 0.2 copy.14
  62.5 0.1 fusion.10
  62.6 0.8 %copy.15 = bf16[128,1024]{1,0:T(8,128)(2,1)} copy(bf16[128,1024]{0,1:T(8,128)(2,1)S(1)} %fusion.10) | data formatting | bytes 524288 | tf_op jit(solution)/shard_map/convert_element_type | solution.py:121
  (5 shorter events, 0.0 us)
Async XLA Ops:
  2.1 15.2 %all-to-all-start = ((bf16[128,4,256]{2,0,1:T(8,128)(2,1)}), bf16[128,4,256]{2,0,1:T(8,128)(2,1)S(1)}, u32[]{:S(2)}, u32[]{:S(2)}) async-start(bf16[128,4,256]{2,0,1:T(8,128)(2,1)} %copy.9), calls=%async_computation | async-start | bytes 524288 | tf_op jit(solution)/shard_map/all_to_all | solution.py:86
  17.3 10.4 %all-to-all-start.1 = ((bf16[128,4,256]{2,0,1:T(8,128)(2,1)}), bf16[128,4,256]{2,0,1:T(8,128)(2,1)S(1)}, u32[]{:S(2)}, u32[]{:S(2)}) async-start(bf16[128,4,256]{2,0,1:T(8,128)(2,1)} %copy.11), calls=%async_computation.1 | async-start | bytes 524288 | tf_op jit(solution)/shard_map/all_to_all | solution.py:85
  29.6 1.2 %copy-start = (f32[4,256,129]{1,2,0:T(8,128)S(1)}, f32[4,256,129]{1,2,0:T(8,128)}, u32[]{:S(2)}) copy-start(f32[4,256,129]{1,2,0:T(8,128)} %fusion.17) | copy-start | bytes 1585156
  45.3 5.2 %copy-start.1 = (bf16[128,1024]{1,0:T(8,128)(2,1)S(1)}, bf16[128,1024]{1,0:T(8,128)(2,1)}, u32[]{:S(2)}) copy-start(bf16[128,1024]{1,0:T(8,128)(2,1)} %param.7) | copy-start | bytes 786436
  47.1 15.2 %all-to-all-start.2 = ((f32[4,128,256]{2,1,0:T(8,128)}), f32[4,128,256]{2,1,0:T(8,128)S(1)}, u32[]{:S(2)}, u32[]{:S(2)}) async-start(f32[4,128,256]{2,1,0:T(8,128)} %fusion.9), calls=%async_computation.2 | async-start | bytes 1048576 | tf_op jit(solution)/shard_map/all_to_all | solution.py:119
where the time goes:
time: 64.1 us; the launch traced here: 63.4 us
  waiting for transfers between devices  23 us (36%)
  starting transfers between devices  13.2 us (21%)
  local copies, waits for them, and re-layouts  10 us (16%)
  matrix products  9.6 us (15%)
  other arithmetic  7.24 us (11%)
    all_to_all x1, waiting for transfers between devices, body(): lax.all_to_all(before_gate, 'ctx', split_axis=0, concat_axis=1, tiled=True)  11.5 us
    all_to_all x1, starting transfers between devices, body(): lax.all_to_all(taps_share, 'ctx', split_axis=1, concat_axis=0, tiled=True)  6.32 us
    add x4, other arithmetic, add_lag(): acc_im = acc_im + coef_re * moved_im + coef_im * moved_re  6.3 us
    all_to_all x1, waiting for transfers between devices, body(): lax.all_to_all(taps_share, 'ctx', split_axis=1, concat_axis=0, tiled=True)  6.21 us
    all_to_all x1, waiting for transfers between devices, body(): lax.all_to_all(value_share, 'ctx', split_axis=1, concat_axis=0, tiled=True)  5.26 us
    mul x4, local copies, waits for them, and re-layouts, add_lag(): acc_re = acc_re + coef_re * moved_re - coef_im * moved_im  3.71 us
    all_to_all x1, starting transfers between devices, body(): lax.all_to_all(before_gate, 'ctx', split_axis=0, concat_axis=1, tiled=True)  3.47 us
    all_to_all x1, starting transfers between devices, body(): lax.all_to_all(value_share, 'ctx', split_axis=1, concat_axis=0, tiled=True)  3.4 us
  transfers between devices with their start and end apart: 3, of which 3 were waited for; matrix products, arithmetic and copies ran while one was open for 7% of the time, Pallas kernels for 0%

commit v1 on v0

v1 whole, which is shorter than its diff:
```python
import functools

import jax
import jax.numpy as jnp
import ml_dtypes
import numpy as np
from jax import lax
from jax.experimental import pallas as pl
from jax.experimental.pallas import tpu as pltpu
from jax.sharding import PartitionSpec as P

LANES = 128
MIB = 1 << 20


def split(table):
    upper = table.astype(ml_dtypes.bfloat16)
    lower = (table - upper.astype(np.float64)).astype(ml_dtypes.bfloat16)
    return upper, lower


def dft_tables(rows):
    length = 2 * rows
    frequency = np.concatenate([np.arange(0, rows, 2), np.arange(1, rows, 2)])
    odd = 2 * frequency[:, None] + 1
    angle = 2.0 * np.pi * (odd * np.arange(rows)[None, :] % (2 * length)) / (2 * length)
    forward = np.concatenate([np.cos(angle), -np.sin(angle)], 0)
    back = np.concatenate([np.cos(angle.T), -np.sin(angle.T)], 1) / rows
    upper, lower = split(back)
    return np.concatenate(split(forward), 1), np.concatenate([upper, lower, upper], 1)


def to(count, me, step):
    return lax.rem(me + step, count)


def came(count, me, step):
    return lax.rem(me - step + count, count)


def ring(count, step):
    return [(i, (i + step) % count) for i in range(count)]


def dot(a, b):
    return jnp.dot(a, b, preferred_element_type=jnp.float32)


def take(values, taps, count, chunks, lanes):
    me = lax.axis_index("ctx")
    first = lax.axis_index("lag") * (count * chunks * lanes)

    def piece(chunk, step):
        start = first + (to(count, me, step) * chunks + chunk) * lanes
        return jnp.concatenate(
            [lax.dynamic_slice_in_dim(array, start, lanes, 1) for array in (values, taps)], 1
        )

    return [[piece(chunk, step) for step in range(count)] for chunk in range(chunks)]


def conv_kernel(count, *refs):
    pieces = refs[:count]
    bias, forward, back = refs[count : count + 3]
    outs = refs[count + 3 : 2 * count + 3]
    blocks, spectrum, total, result = refs[2 * count + 3 :]
    rows, lanes = outs[0].shape
    me = lax.axis_index("ctx")
    table = forward[...]
    for step in range(count):
        i = came(count, me, step)
        x = pieces[step][...]
        blocks[i] = x[:, :lanes]
        spectrum[i] = dot(table, jnp.concatenate([x, x], 0))

    def tile(t, sign):
        re = pl.ds(pl.multiple_of(t * 8, 8), 8)
        im = pl.ds(pl.multiple_of(rows + t * 8, 8), 8)
        val_re = [spectrum[i, re, :lanes] for i in range(count)]
        val_im = [spectrum[i, im, :lanes] for i in range(count)]
        tap_re = [spectrum[i, re, lanes:] for i in range(count)]
        tap_im = [spectrum[i, im, lanes:] for i in range(count)]
        last_re = last_im = 0.0
        for r in range(count):
            sum_re = sum_im = 0.0
            for i in range(r + 1):
                a, b, c, d = val_re[i], val_im[i], tap_re[r - i], tap_im[r - i]
                sum_re = sum_re + (a * c - b * d)
                sum_im = sum_im + (a * d + b * c)
            total[r, re, :] = sum_re - sign * last_im
            total[r, im, :] = sum_im + sign * last_re
            last_re, last_im = sum_re, sum_im

    half = rows // 16
    pl.loop(0, half)(lambda t: tile(t, 1.0))
    pl.loop(half, 2 * half)(lambda t: tile(t, -1.0))

    for r in range(count):
        y = total[r]
        upper = y.astype(jnp.bfloat16)
        lower = (y - upper.astype(jnp.float32)).astype(jnp.bfloat16)
        conv = dot(back[...], jnp.concatenate([upper, upper, lower], 0))
        skip = bias[...] * blocks[r].astype(jnp.float32)
        result[r] = (conv + skip).astype(jnp.bfloat16)
    for step in range(count):
        outs[step][...] = result[to(count, me, step)]


def convolve(arrived, bias, forward, back):
    count = len(arrived)
    rows, lanes = arrived[0].shape[0], arrived[0].shape[1] // 2
    vmem = pl.BlockSpec(memory_space=pltpu.VMEM)
    return pl.pallas_call(
        functools.partial(conv_kernel, count),
        out_shape=[jax.ShapeDtypeStruct((rows, lanes), jnp.bfloat16)] * count,
        in_specs=[vmem] * (count + 3),
        out_specs=[vmem] * count,
        scratch_shapes=[
            pltpu.VMEM((count, rows, lanes), jnp.bfloat16),
            pltpu.VMEM((count, 2 * rows, 2 * lanes), jnp.float32),
            pltpu.VMEM((count, 2 * rows, lanes), jnp.float32),
            pltpu.VMEM((count, rows, lanes), jnp.bfloat16),
        ],
        compiler_params=pltpu.CompilerParams(vmem_limit_bytes=16 * MIB),
        name="convolve",
    )(*arrived, bias, forward, back)


def gate_kernel(count, chunks, lanes, *refs):
    pieces, gate, out = refs[:-2], refs[-2], refs[-1]
    me = lax.axis_index("ctx")
    for step in range(count):
        owner = came(count, me, step)
        for chunk in range(chunks):
            cols = pl.ds(pl.multiple_of((owner * chunks + chunk) * lanes, LANES), lanes)
            mixed = gate[:, cols].astype(jnp.float32) * pieces[chunk * count + step][...].astype(
                jnp.float32
            )
            out[:, cols] = mixed.astype(jnp.bfloat16)


def apply_gate(returned, gate):
    chunks, count = len(returned), len(returned[0])
    lanes = returned[0][0].shape[1]
    pieces = [piece for group in returned for piece in group]
    if lanes % LANES == 0:
        vmem = pl.BlockSpec(memory_space=pltpu.VMEM)
        return pl.pallas_call(
            functools.partial(gate_kernel, count, chunks, lanes),
            out_shape=jax.ShapeDtypeStruct(gate.shape, jnp.bfloat16),
            in_specs=[vmem] * (len(pieces) + 1),
            out_specs=vmem,
            compiler_params=pltpu.CompilerParams(vmem_limit_bytes=2 * MIB),
            name="gate",
        )(*pieces, gate)
    me = lax.axis_index("ctx")
    stacked = jnp.stack(pieces).reshape(chunks, count, gate.shape[0], lanes)
    ordered = jnp.roll(stacked[:, ::-1], me + 1, 1)
    whole = jnp.transpose(ordered, (2, 1, 0, 3)).reshape(gate.shape)
    return (gate.astype(jnp.float32) * whole.astype(jnp.float32)).astype(jnp.bfloat16)


def exchange(pieces):
    count = len(pieces)
    return [pieces[0]] + [
        lax.ppermute(pieces[step], "ctx", ring(count, step))
        for step in range(1, count)
    ]


def body(values, gate, bias, filter_taps):
    rows, share = gate.shape
    count = lax.axis_size("ctx")
    narrow = share // count
    lanes = narrow if narrow % LANES else LANES * 2
    chunks = narrow // lanes
    forward, back = (jnp.asarray(table) for table in dft_tables(rows))
    first = (lax.axis_index("lag") * count + lax.axis_index("ctx")) * narrow
    own_bias = lax.dynamic_slice_in_dim(bias, first, narrow, 0).reshape(chunks, 1, lanes)
    pieces = take(values, filter_taps, count, chunks, lanes)
    arrived = [exchange(group) for group in pieces]
    returned = [
        exchange(convolve(group, own_bias[chunk], forward, back))
        for chunk, group in enumerate(arrived)
    ]
    return apply_gate(returned, gate)


def solution(mesh):
    return jax.shard_map(
        body,
        mesh=mesh,
        in_specs=(P("ctx", "chan"), P("ctx", ("chan", "lag")), P("chan"), P("ctx", "chan")),
        out_specs=P("ctx", ("chan", "lag")),
        check_vma=False,
    )
```

time: 64.1 us -> 27 us (0.42)
  waiting for transfers between devices: 23 us -> 8.02 us
  matrix products: 9.6 us -> 0 us
  local copies, waits for them, and re-layouts: 10 us -> 1.88 us
  other arithmetic: 7.24 us -> 0.04 us
  Pallas kernels: 0 us -> 2.13 us
  starting transfers between devices: 13.2 us -> 14.7 us
    all_to_all x3 -> x0, waiting for transfers between devices: 23 us -> none  [the longest x1 11.5 us: body(): lax.all_to_all(before_gate, 'ctx', split_axis=0, concat_axis=1, tiled=True)]
    ppermute x0 -> x6, starting transfers between devices: none -> 14.7 us  [exchange(): lax.ppermute(pieces[step], 'ctx', ring(count, step))]
    all_to_all x3 -> x0, starting transfers between devices: 13.2 us -> none  [the longest x1 6.32 us: body(): lax.all_to_all(taps_share, 'ctx', split_axis=1, concat_axis=0, tiled=True)]
    dot_general x14 -> x0, matrix products: 9.6 us -> none  [the longest x3 2.17 us: transform(): jnp.einsum('fm,...mc->...fc', cos_parts[1], operand, preferred_element_ty...]
    ppermute x0 -> x6, waiting for transfers between devices: none -> 8.02 us  [exchange(): lax.ppermute(pieces[step], 'ctx', ring(count, step))]
    add x5 -> x0, other arithmetic: 6.31 us -> none  [the longest x4 6.3 us: add_lag(): acc_im = acc_im + coef_re * moved_im + coef_im * moved_re]
    mul x4 -> x0, local copies, waits for them, and re-layouts: 3.71 us -> none  [add_lag(): acc_re = acc_re + coef_re * moved_re - coef_im * moved_im]
    pallas_call x0 -> x2, Pallas kernels: none -> 2.13 us  [the longest x1 1.35 us: convolve(): pl.pallas_call(functools.partial(conv_kernel, count), out_shape=[jax.Shap...]
  transfers between devices with their start and end apart: 3 -> 6, of which waited for: 3 -> 3; matrix products, arithmetic and copies ran while one was open for 7% -> 3% of each run, Pallas kernels for 0% -> 0%
where the time goes in v1:
time: 27 us; the launch traced here: 26.8 us
  starting transfers between devices  14.7 us (54%)
  waiting for transfers between devices  8.02 us (30%)
  Pallas kernels  2.13 us (8%)
  local copies, waits for them, and re-layouts  1.88 us (7%)
    ppermute x6, starting transfers between devices, exchange(): lax.ppermute(pieces[step], 'ctx', ring(count, step))  14.7 us
    ppermute x6, waiting for transfers between devices, exchange(): lax.ppermute(pieces[step], 'ctx', ring(count, step))  8.02 us
    pallas_call x1, Pallas kernels, convolve(): pl.pallas_call(functools.partial(conv_kernel, count), out_shape=[jax.Shap...  1.35 us
    dynamic_slice x1, local copies, waits for them, and re-layouts, piece(): lax.dynamic_slice_in_dim(array, start, lanes, 1)  1.1 us
    pallas_call x1, Pallas kernels, apply_gate(): pl.pallas_call(functools.partial(gate_kernel, count, chunks, lanes), out_...  0.78 us
    dynamic_slice x1, local copies, waits for them, and re-layouts, body(): lax.dynamic_slice_in_dim(bias, first, narrow, 0).reshape(chunks, 1, lanes)  0.76 us
  transfers between devices with their start and end apart: 6, of which 3 were waited for; matrix products, arithmetic and copies ran while one was open for 3% of the time, Pallas kernels for 0%

profile of v1, /device:TPU:0, one launch (start us, length us, event | category | flops | bytes accessed | tf_op | source)
XLA Modules:
  0.0 26.8 jit_solution(7433217293085871634)
XLA Ops:
  0.0 1.1 %constant_dynamic-slice_fusion = (bf16[128,256]{1,0:T(8,128)(2,1)S(1)}, bf16[128,256]{1,0:T(8,128)(2,1)S(1)}, bf16[128,256]{1,0:T(8,128)(2,1)S(1)}, bf16[128,256...) fusion(bf16[128,4096]{1,0:T(8,128)(2,1)} %param.9, ...), kind=kLoop, calls=%fused_computation.4 | loop fusion | bytes 1048592 | tf_op jit(solution)/shard_map/dynamic_slice | solution.py:56
  1.1 4.1 %collective-permute-start.1 = (bf16[128,512]{1,0:T(8,128)(2,1)S(1)}, bf16[128,512]{1,0:T(8,128)(2,1)S(1)}, u32[]{:S(2)}, u32[]{:S(2)}) collective-permute-start(bf16[128,512]{1,0:T(8,128)(2,1)S(1)} %pad_maximum_fusion.2), channel_id=1, source_target_pairs={{0,16},{8,24},{16,0},{24,8},{1,17},{9,25},{17,1},{25,9},{2,18},{10... | collective-permute-start | bytes 393224 | tf_op jit(solution)/shard_map/ppermute | solution.py:166
  5.2 1.6 %collective-permute-start = (bf16[128,512]{1,0:T(8,128)(2,1)S(1)}, bf16[128,512]{1,0:T(8,128)(2,1)S(1)}, u32[]{:S(2)}, u32[]{:S(2)}) collective-permute-start(bf16[128,512]{1,0:T(8,128)(2,1)S(1)} %pad_maximum_fusion.1), channel_id=1, source_target_pairs={{0,8},{8,16},{16,24},{24,0},{1,9},{9,17},{17,25},{25,1},{2,10},{10... | collective-permute-start | bytes 393224 | tf_op jit(solution)/shard_map/ppermute | solution.py:166
  6.9 0.0 copy-start.2
  6.9 0.0 copy-start.1
  6.9 2.3 %collective-permute-start.2 = (bf16[128,512]{1,0:T(8,128)(2,1)S(1)}, bf16[128,512]{1,0:T(8,128)(2,1)S(1)}, u32[]{:S(2)}, u32[]{:S(2)}) collective-permute-start(bf16[128,512]{1,0:T(8,128)(2,1)S(1)} %pad_maximum_fusion.3), channel_id=1, source_target_pairs={{0,24},{8,0},{16,8},{24,16},{1,25},{9,1},{17,9},{25,17},{2,26},{10... | collective-permute-start | bytes 393224 | tf_op jit(solution)/shard_map/ppermute | solution.py:166
  9.2 0.8 %dynamic_slice.35 = f32[256]{0:T(256)S(1)} dynamic-slice(f32[4096]{0:T(1024)} %param.8, s32[]{:T(128)S(6)} %select_n.23), dynamic_slice_sizes={256} | dynamic-slice | bytes 2052 | tf_op jit(solution)/shard_map/dynamic_slice | solution.py:179
  10.0 5.2 %collective-permute-done.1.refs_2_ = bf16[128,512]{1,0:T(8,128)(2,1)S(1)} collective-permute-done((bf16[128,512]{1,0:T(8,128)(2,1)S(1)}, bf16[128,512]{1,0:T(8,128)(2,1)S(1)}, u32[]{:S(2)}, u32[]{:S(2)}) %collective-permute-start.1) | collective-permute-done | bytes 131104 | tf_op jit(solution)/shard_map/ppermute | solution.py:166
  15.2 0.0 collective-permute-done.refs_1_
  15.2 0.9 %collective-permute-done.2.refs_3_ = bf16[128,512]{1,0:T(8,128)(2,1)S(1)} collective-permute-done((bf16[128,512]{1,0:T(8,128)(2,1)S(1)}, bf16[128,512]{1,0:T(8,128)(2,1)S(1)}, u32[]{:S(2)}, u32[]{:S(2)}) %collective-permute-start.2) | collective-permute-done | bytes 131104 | tf_op jit(solution)/shard_map/ppermute | solution.py:166
  16.1 0.0 copy-done.2
  16.1 0.0 copy-done.1
  16.1 0.0 copy-start
  16.1 1.3 %convolve.1 = (bf16[128,256]{1,0:T(8,128)(2,1)S(1)}, bf16[128,256]{1,0:T(8,128)(2,1)S(1)}, bf16[128,256]{1,0:T(8,128)(2,1)S(1)}, bf16[128,256]{1,0:T(8,128)(2,1)S(1)}) custom-call(bf16[128,512]{1,0:T(8,128)(2,1)S(1)} %pad_maximum_fusion.refs_0_, bf16[128,512]{1,0:T(8,128)(2,1)S(1)} %collective-permute-done.refs_1_, ...), custom_call_target="tpu_custom_call" | custom-call | tf_op jit(solution)/shard_map/convolve/pallas_call | solution.py:113
  17.4 1.9 %collective-permute-start.3 = (bf16[128,256]{1,0:T(8,128)(2,1)S(1)}, bf16[128,256]{1,0:T(8,128)(2,1)S(1)}, u32[]{:S(2)}, u32[]{:S(2)}) collective-permute-start(bf16[128,256]{1,0:T(8,128)(2,1)S(1)} %get-tuple-element.10), channel_id=1, source_target_pairs={{0,8},{8,16},{16,24},{24,0},{1,9},{9,17},{17,25},{25,1},{2,10},{10... | collective-permute-start | bytes 196616 | tf_op jit(solution)/shard_map/ppermute | solution.py:166
  19.3 2.0 %collective-permute-start.4 = (bf16[128,256]{1,0:T(8,128)(2,1)S(1)}, bf16[128,256]{1,0:T(8,128)(2,1)S(1)}, u32[]{:S(2)}, u32[]{:S(2)}) collective-permute-start(bf16[128,256]{1,0:T(8,128)(2,1)S(1)} %get-tuple-element.11), channel_id=1, source_target_pairs={{0,16},{8,24},{16,0},{24,8},{1,17},{9,25},{17,1},{25,9},{2,18},{10... | collective-permute-start | bytes 196616 | tf_op jit(solution)/shard_map/ppermute | solution.py:166
  21.3 2.8 %collective-permute-start.5 = (bf16[128,256]{1,0:T(8,128)(2,1)S(1)}, bf16[128,256]{1,0:T(8,128)(2,1)S(1)}, u32[]{:S(2)}, u32[]{:S(2)}) collective-permute-start(bf16[128,256]{1,0:T(8,128)(2,1)S(1)} %get-tuple-element.12), channel_id=1, source_target_pairs={{0,24},{8,0},{16,8},{24,16},{1,25},{9,1},{17,9},{25,17},{2,26},{10... | collective-permute-start | bytes 196616 | tf_op jit(solution)/shard_map/ppermute | solution.py:166
  24.2 0.0 collective-permute-done.3.refs_1_
  24.2 1.9 %collective-permute-done.4.refs_2_ = bf16[128,256]{1,0:T(8,128)(2,1)S(1)} collective-permute-done((bf16[128,256]{1,0:T(8,128)(2,1)S(1)}, bf16[128,256]{1,0:T(8,128)(2,1)S(1)}, u32[]{:S(2)}, u32[]{:S(2)}) %collective-permute-start.4) | collective-permute-done | bytes 65568 | tf_op jit(solution)/shard_map/ppermute | solution.py:166
  26.1 0.0 collective-permute-done.5.refs_3_
  26.1 0.0 copy-done
  26.1 0.8 %gate.1 = bf16[128,1024]{1,0:T(8,128)(2,1)} custom-call(bf16[128,256]{1,0:T(8,128)(2,1)S(1)} %get-tuple-element.9.refs_0_, bf16[128,256]{1,0:T(8,128)(2,1)S(1)} %collective-permute-done.3.refs_1_, bf16[128,256]{1,0:T(8,128)(2,1)S(1)} %collective-permute-done.4.refs_2_, bf16[128,256]{1,0:T(8,128)(2,1)S(1)} %collective-permute-done.5.refs_3_, ...), custom_call_target="tpu_custom_call" | custom-call | tf_op jit(solution)/shard_map/gate/pallas_call | solution.py:148
  (4 shorter events, 0.0 us)
Async XLA Ops:
  1.1 14.1 %collective-permute-start.1 = (bf16[128,512]{1,0:T(8,128)(2,1)S(1)}, bf16[128,512]{1,0:T(8,128)(2,1)S(1)}, u32[]{:S(2)}, u32[]{:S(2)}) collective-permute-start(bf16[128,512]{1,0:T(8,128)(2,1)S(1)} %pad_maximum_fusion.2), channel_id=1, source_target_pairs={{0,16},{8,24},{16,0},{24,8},{1,17},{9,25},{17,1},{25,9},{2,18},{10... | collective-permute-start | bytes 393224 | tf_op jit(solution)/shard_map/ppermute | solution.py:166
  5.2 10.0 %collective-permute-start = (bf16[128,512]{1,0:T(8,128)(2,1)S(1)}, bf16[128,512]{1,0:T(8,128)(2,1)S(1)}, u32[]{:S(2)}, u32[]{:S(2)}) collective-permute-start(bf16[128,512]{1,0:T(8,128)(2,1)S(1)} %pad_maximum_fusion.1), channel_id=1, source_target_pairs={{0,8},{8,16},{16,24},{24,0},{1,9},{9,17},{17,25},{25,1},{2,10},{10... | collective-permute-start | bytes 393224 | tf_op jit(solution)/shard_map/ppermute | solution.py:166
  6.9 9.2 %copy-start.2 = (bf16[256,256]{1,0:T(8,128)(2,1)S(1)}, bf16[256,256]{1,0:T(8,128)(2,1)}, u32[]{:S(2)}) copy-start(bf16[256,256]{1,0:T(8,128)(2,1)} %constant.37.clone.refs_5_) | copy-start | bytes 393220
  6.9 9.2 %copy-start.1 = (bf16[128,768]{1,0:T(8,128)(2,1)S(1)}, bf16[128,768]{1,0:T(8,128)(2,1)}, u32[]{:S(2)}) copy-start(bf16[128,768]{1,0:T(8,128)(2,1)} %constant.38.clone.refs_6_) | copy-start | bytes 589828
  6.9 9.2 %collective-permute-start.2 = (bf16[128,512]{1,0:T(8,128)(2,1)S(1)}, bf16[128,512]{1,0:T(8,128)(2,1)S(1)}, u32[]{:S(2)}, u32[]{:S(2)}) collective-permute-start(bf16[128,512]{1,0:T(8,128)(2,1)S(1)} %pad_maximum_fusion.3), channel_id=1, source_target_pairs={{0,24},{8,0},{16,8},{24,16},{1,25},{9,1},{17,9},{25,17},{2,26},{10... | collective-permute-start | bytes 393224 | tf_op jit(solution)/shard_map/ppermute | solution.py:166
  16.1 10.0 %copy-start = (bf16[128,1024]{1,0:T(8,128)(2,1)S(1)}, bf16[128,1024]{1,0:T(8,128)(2,1)}, u32[]{:S(2)}) copy-start(bf16[128,1024]{1,0:T(8,128)(2,1)} %refs_4_.1) | copy-start | bytes 786436
  17.4 6.7 %collective-permute-start.3 = (bf16[128,256]{1,0:T(8,128)(2,1)S(1)}, bf16[128,256]{1,0:T(8,128)(2,1)S(1)}, u32[]{:S(2)}, u32[]{:S(2)}) collective-permute-start(bf16[128,256]{1,0:T(8,128)(2,1)S(1)} %get-tuple-element.10), channel_id=1, source_target_pairs={{0,8},{8,16},{16,24},{24,0},{1,9},{9,17},{17,25},{25,1},{2,10},{10... | collective-permute-start | bytes 196616 | tf_op jit(solution)/shard_map/ppermute | solution.py:166
  19.3 6.8 %collective-permute-start.4 = (bf16[128,256]{1,0:T(8,128)(2,1)S(1)}, bf16[128,256]{1,0:T(8,128)(2,1)S(1)}, u32[]{:S(2)}, u32[]{:S(2)}) collective-permute-start(bf16[128,256]{1,0:T(8,128)(2,1)S(1)} %get-tuple-element.11), channel_id=1, source_target_pairs={{0,16},{8,24},{16,0},{24,8},{1,17},{9,25},{17,1},{25,9},{2,18},{10... | collective-permute-start | bytes 196616 | tf_op jit(solution)/shard_map/ppermute | solution.py:166
  21.3 4.8 %collective-permute-start.5 = (bf16[128,256]{1,0:T(8,128)(2,1)S(1)}, bf16[128,256]{1,0:T(8,128)(2,1)S(1)}, u32[]{:S(2)}, u32[]{:S(2)}) collective-permute-start(bf16[128,256]{1,0:T(8,128)(2,1)S(1)} %get-tuple-element.12), channel_id=1, source_target_pairs={{0,24},{8,0},{16,8},{24,16},{1,25},{9,1},{17,9},{25,17},{2,26},{10... | collective-permute-start | bytes 196616 | tf_op jit(solution)/shard_map/ppermute | solution.py:166

commit v2 on v1

v2 whole, which is shorter than its diff:
```python
import functools

import jax
import jax.numpy as jnp
import ml_dtypes
import numpy as np
from jax import lax
from jax.experimental import pallas as pl
from jax.experimental.pallas import tpu as pltpu
from jax.sharding import PartitionSpec as P

LANES = 128
MIB = 1 << 20
VMEM = pl.BlockSpec(memory_space=pltpu.VMEM)
OUT = ("swap", 2, 1, 3)
BACK = ("ring", 1, 2, 3)


def split(table):
    upper = table.astype(ml_dtypes.bfloat16)
    lower = (table - upper.astype(np.float64)).astype(ml_dtypes.bfloat16)
    return upper, lower


def dft_tables(rows):
    length = 2 * rows
    frequency = np.concatenate([np.arange(0, rows, 2), np.arange(1, rows, 2)])
    odd = 2 * frequency[:, None] + 1
    angle = 2.0 * np.pi * (odd * np.arange(rows)[None, :] % (2 * length)) / (2 * length)
    forward = np.concatenate([np.cos(angle), -np.sin(angle)], 0)
    back = np.concatenate([np.cos(angle.T), -np.sin(angle.T)], 1) / rows
    upper, lower = split(back)
    return np.concatenate(split(forward), 1), np.concatenate([upper, lower, upper], 1)


def steps(plan, count):
    return list(plan[1:]) if count == 4 else list(range(1, count))


def swaps(plan, count):
    return plan[0] == "swap" and count & (count - 1) == 0


def to(plan, count, me, step):
    return me ^ step if swaps(plan, count) else lax.rem(me + step, count)


def came(plan, count, me, step):
    return me ^ step if swaps(plan, count) else lax.rem(me - step + count, count)


def pairs(plan, count, step):
    if swaps(plan, count):
        return [(i, i ^ step) for i in range(count)]
    return [(i, (i + step) % count) for i in range(count)]


def dot(a, b):
    return jnp.dot(a, b, preferred_element_type=jnp.float32)


def take(values, taps, count, lanes):
    me = lax.axis_index("ctx")
    first = lax.axis_index("lag") * (count * lanes)
    later = lax.optimization_barrier((values, taps))

    def piece(step, arrays):
        start = first + to(OUT, count, me, step) * lanes
        return jnp.concatenate(
            [lax.dynamic_slice_in_dim(array, start, lanes, 1) for array in arrays], 1
        )

    order = steps(OUT, count)
    pieces = {step: piece(step, (values, taps) if step == order[0] else later) for step in order}
    return piece(0, later), [pieces[step] for step in order]


def transform_into(plan, step, piece, table, spectra):
    count = spectra.shape[0]
    x = piece[...]
    owner = came(plan, count, lax.axis_index("ctx"), step)
    spectra[owner] = dot(table[...], jnp.concatenate([x, x], 0))


def transform_kernel(step, *refs):
    piece, table, spectra = refs[0], refs[1], refs[-1]
    transform_into(OUT, step, piece, table, spectra)


def transform(spectra, step, piece, table, count):
    shape = jax.ShapeDtypeStruct((count, table.shape[0], piece.shape[1]), jnp.float32)
    held = [] if spectra is None else [spectra]
    return pl.pallas_call(
        functools.partial(transform_kernel, step),
        out_shape=shape,
        in_specs=[VMEM] * (2 + len(held)),
        out_specs=VMEM,
        input_output_aliases={2: 0} if held else {},
        compiler_params=pltpu.CompilerParams(vmem_limit_bytes=2 * MIB),
        cost_estimate=pl.CostEstimate(
            flops=2 * table.size * piece.shape[1],
            bytes_accessed=8 * piece.size,
            transcendentals=0,
        ),
        name="transform",
    )(piece, table, *held)


def conv_kernel(count, step, piece, bias, forward, back, _, spectra, *refs):
    outs, total, result = refs[:count], refs[count], refs[count + 1]
    rows, lanes = outs[0].shape
    me = lax.axis_index("ctx")
    transform_into(OUT, step, piece, forward, spectra)
    width = min(lanes, LANES)
    base = 0
    if lanes % LANES == 0:
        base = pl.multiple_of((lax.axis_index("lag") * count + me) * lanes, LANES)

    def tile(t, sign):
        re = pl.ds(pl.multiple_of(t * 8, 8), 8)
        im = pl.ds(pl.multiple_of(rows + t * 8, 8), 8)
        for first in range(0, lanes, width):
            val = slice(first, first + width)
            tap = slice(lanes + first, lanes + first + width)
            val_re = [spectra[i, re, val] for i in range(count)]
            val_im = [spectra[i, im, val] for i in range(count)]
            tap_re = [spectra[i, re, tap] for i in range(count)]
            tap_im = [spectra[i, im, tap] for i in range(count)]
            tap_re[0] = tap_re[0] + bias[:, pl.ds(base + first, width)]
            last_re = last_im = 0.0
            for r in range(count):
                sum_re = sum_im = 0.0
                for i in range(r + 1):
                    a, b, c, d = val_re[i], val_im[i], tap_re[r - i], tap_im[r - i]
                    sum_re = sum_re + (a * c - b * d)
                    sum_im = sum_im + (a * d + b * c)
                total[r, re, val] = sum_re - sign * last_im
                total[r, im, val] = sum_im + sign * last_re
                last_re, last_im = sum_re, sum_im

    half = rows // 16
    unroll = half if count <= 4 else 1
    pl.loop(0, half, unroll=unroll)(lambda t: tile(t, 1.0))
    pl.loop(half, 2 * half, unroll=unroll)(lambda t: tile(t, -1.0))

    for r in range(count):
        y = total[r]
        upper = y.astype(jnp.bfloat16)
        lower = (y - upper.astype(jnp.float32)).astype(jnp.bfloat16)
        conv = dot(back[...], jnp.concatenate([upper, upper, lower], 0))
        result[r] = conv.astype(jnp.bfloat16)
    for place, step_back in enumerate([0] + steps(BACK, count)):
        outs[place][...] = result[to(BACK, count, me, step_back)]


def convolve(spectra, step, piece, bias, forward, back):
    count, length, both = spectra.shape
    rows, lanes = length // 2, both // 2
    outs = pl.pallas_call(
        functools.partial(conv_kernel, count, step),
        out_shape=[jax.ShapeDtypeStruct(spectra.shape, jnp.float32)]
        + [jax.ShapeDtypeStruct((rows, lanes), jnp.bfloat16)] * count,
        in_specs=[VMEM] * 5,
        out_specs=[VMEM] * (count + 1),
        scratch_shapes=[
            pltpu.VMEM((count, length, lanes), jnp.float32),
            pltpu.VMEM((count, rows, lanes), jnp.bfloat16),
        ],
        input_output_aliases={4: 0},
        compiler_params=pltpu.CompilerParams(vmem_limit_bytes=8 * MIB),
        name="convolve",
    )(piece, bias, forward, back, spectra)
    return outs[1:]


def gate_kernel(count, lanes, *refs):
    pieces, gate, out = refs[:count], refs[count], refs[count + 1]
    me = lax.axis_index("ctx")
    for place, step in enumerate([0] + steps(BACK, count)):
        cols = pl.ds(pl.multiple_of(came(BACK, count, me, step) * lanes, LANES), lanes)
        mixed = gate[:, cols].astype(jnp.float32) * pieces[place][...].astype(jnp.float32)
        out[:, cols] = mixed.astype(jnp.bfloat16)


def apply_gate(returned, gate):
    count = len(returned)
    lanes = returned[0].shape[1]
    if lanes % LANES == 0:
        return pl.pallas_call(
            functools.partial(gate_kernel, count, lanes),
            out_shape=jax.ShapeDtypeStruct(gate.shape, jnp.bfloat16),
            in_specs=[VMEM] * (count + 1),
            out_specs=VMEM,
            compiler_params=pltpu.CompilerParams(vmem_limit_bytes=2 * MIB),
            name="gate",
        )(*returned, gate)
    me = lax.axis_index("ctx")
    ordered = jnp.roll(jnp.stack(returned)[::-1], me + 1, 0)
    whole = jnp.transpose(ordered, (1, 0, 2)).reshape(gate.shape)
    return (gate.astype(jnp.float32) * whole.astype(jnp.float32)).astype(jnp.bfloat16)


def move(plan, count, step, piece):
    return lax.ppermute(piece, "ctx", pairs(plan, count, step))


def body(values, gate, bias, filter_taps):
    rows, share = gate.shape
    count = lax.axis_size("ctx")
    lanes = share // count
    forward, back = (jnp.asarray(table) for table in dft_tables(rows))
    own_bias = bias.reshape(1, -1)
    if lanes % LANES:
        start = (lax.axis_index("lag") * count + lax.axis_index("ctx")) * lanes
        own_bias = lax.dynamic_slice_in_dim(own_bias, start, lanes, 1)
    own, pieces = take(values, filter_taps, count, lanes)
    out_steps, back_steps = steps(OUT, count), steps(BACK, count)
    arrived = [move(OUT, count, step, piece) for step, piece in zip(out_steps, pieces)]
    spectra = transform(None, 0, own, forward, count)
    for step, piece in zip(out_steps[:-1], arrived):
        spectra = transform(spectra, step, piece, forward, count)
    done = convolve(spectra, out_steps[-1], arrived[-1], own_bias, forward, back)
    returned = [move(BACK, count, step, piece) for step, piece in zip(back_steps, done[1:])]
    return apply_gate([done[0]] + returned, gate)


def solution(mesh):
    return jax.shard_map(
        body,
        mesh=mesh,
        in_specs=(P("ctx", "chan"), P("ctx", ("chan", "lag")), P("chan"), P("ctx", "chan")),
        out_specs=P("ctx", ("chan", "lag")),
        check_vma=False,
    )
```

time: 27 us -> 26.6 us (0.985)
  starting transfers between devices: 14.7 us -> 12.6 us
  waiting for transfers between devices: 8.02 us -> 9.17 us
  Pallas kernels: 2.13 us -> 2.48 us
    ppermute x6, starting transfers between devices: 14.7 us -> 12.6 us  [move(): return lax.ppermute(piece, 'ctx', pairs(plan, count, step))]
    ppermute x6, waiting for transfers between devices: 8.02 us -> 9.17 us  [move(): return lax.ppermute(piece, 'ctx', pairs(plan, count, step))]
    dynamic_slice x1 -> x2, local copies, waits for them, and re-layouts: 1.1 us -> 1.95 us  [piece(): lax.dynamic_slice_in_dim(array, start, lanes, 1)]
    dynamic_slice x1 -> x0, local copies, waits for them, and re-layouts: 0.76 us -> none  [body(): lax.dynamic_slice_in_dim(bias, first, narrow, 0).reshape(chunks, 1, lanes)]
    pallas_call x2 -> x5, Pallas kernels: 2.13 us -> 2.48 us  [the longest x1 1.05 us: convolve(): pl.pallas_call(functools.partial(conv_kernel, count, step), out_shape=[ja...]
  transfers between devices with their start and end apart: 6 -> 6, of which waited for: 3 -> 3; matrix products, arithmetic and copies ran while one was open for 3% -> 4% of each run, Pallas kernels for 0% -> 2%
where the time goes in v2:
time: 26.6 us; the launch traced here: 26.4 us
  starting transfers between devices  12.6 us (47%)
  waiting for transfers between devices  9.17 us (34%)
  Pallas kernels  2.48 us (9%)
  local copies, waits for them, and re-layouts  1.97 us (7%)
    ppermute x6, starting transfers between devices, move(): return lax.ppermute(piece, 'ctx', pairs(plan, count, step))  12.6 us
    ppermute x6, waiting for transfers between devices, move(): return lax.ppermute(piece, 'ctx', pairs(plan, count, step))  9.17 us
    dynamic_slice x2, local copies, waits for them, and re-layouts, piece(): lax.dynamic_slice_in_dim(array, start, lanes, 1)  1.95 us
    pallas_call x1, Pallas kernels, convolve(): pl.pallas_call(functools.partial(conv_kernel, count, step), out_shape=[ja...  1.05 us
    pallas_call x1, Pallas kernels, apply_gate(): pl.pallas_call(functools.partial(gate_kernel, count, lanes), out_shape=ja...  0.78 us
    pallas_call x3, Pallas kernels, transform(): pl.pallas_call(functools.partial(transform_kernel, step), out_shape=shape...  0.65 us
  transfers between devices with their start and end apart: 6, of which 3 were waited for; matrix products, arithmetic and copies ran while one was open for 4% of the time, Pallas kernels for 2%

profile of v2, /device:TPU:0, one launch (start us, length us, event | category | flops | bytes accessed | tf_op | source)
XLA Modules:
  0.0 26.4 jit_solution(11730912599281540587)
XLA Ops:
  0.0 0.0 copy-start
  0.0 0.9 %constant_dynamic-slice_fusion.2 = (bf16[128,256]{1,0:T(8,128)(2,1)S(1)}, bf16[128,256]{1,0:T(8,128)(2,1)S(1)}) fusion(bf16[128,4096]{1,0:T(8,128)(2,1)} %param.9, s32[]{:T(128)S(6)} %select_n.18, bf16[128,4096]{1,0:T(8,128)(2,1)} %param.6), kind=kLoop, calls=%fused_computation.6 | loop fusion | bytes 262148 | tf_op jit(solution)/shard_map/dynamic_slice | solution.py:70
  0.9 4.1 %collective-permute-start.2 = (bf16[128,512]{1,0:T(8,128)(2,1)S(1)}, bf16[128,512]{1,0:T(8,128)(2,1)S(1)}, u32[]{:S(2)}, u32[]{:S(2)}) collective-permute-start(bf16[128,512]{1,0:T(8,128)(2,1)S(1)} %pad_maximum_fusion.2), channel_id=1, source_target_pairs={{0,16},{8,24},{16,0},{24,8},{1,17},{9,25},{17,1},{25,9},{2,18},{10... | collective-permute-start | bytes 393224 | tf_op jit(solution)/shard_map/ppermute | solution.py:204
  5.0 1.0 %constant_dynamic-slice_fusion = (bf16[128,256]{1,0:T(8,128)(2,1)S(1)}, bf16[128,256]{1,0:T(8,128)(2,1)S(1)}, bf16[128,256]{1,0:T(8,128)(2,1)S(1)}, bf16[128,256...) fusion(bf16[128,4096]{1,0:T(8,128)(2,1)} %param.9, s32[]{:T(128)S(6)} %select_n.19, ...), kind=kLoop, calls=%fused_computation.4 | loop fusion | bytes 786444 | tf_op jit(solution)/shard_map/dynamic_slice | solution.py:70
  6.1 1.6 %collective-permute-start.1 = (bf16[128,512]{1,0:T(8,128)(2,1)S(1)}, bf16[128,512]{1,0:T(8,128)(2,1)S(1)}, u32[]{:S(2)}, u32[]{:S(2)}) collective-permute-start(bf16[128,512]{1,0:T(8,128)(2,1)S(1)} %pad_maximum_fusion.1), channel_id=1, source_target_pairs={{0,8},{8,0},{16,24},{24,16},{1,9},{9,1},{17,25},{25,17},{2,10},{10... | collective-permute-start | bytes 393224 | tf_op jit(solution)/shard_map/ppermute | solution.py:204
  7.7 0.1 collective-permute-start
  7.8 0.0 copy-done
  7.9 0.2 transform.3.refs_2_
  8.1 4.7 %collective-permute-done.2.refs_0_ = bf16[128,512]{1,0:T(8,128)(2,1)S(1)} collective-permute-done((bf16[128,512]{1,0:T(8,128)(2,1)S(1)}, bf16[128,512]{1,0:T(8,128)(2,1)S(1)}, u32[]{:S(2)}, u32[]{:S(2)}) %collective-permute-start.2) | collective-permute-done | bytes 131104 | tf_op jit(solution)/shard_map/ppermute | solution.py:204
  12.8 0.2 transform.4.refs_2_
  13.0 0.0 copy-start.2
  13.0 0.0 copy-start.3
  13.1 2.5 %collective-permute-done.1.refs_0_ = bf16[128,512]{1,0:T(8,128)(2,1)S(1)} collective-permute-done((bf16[128,512]{1,0:T(8,128)(2,1)S(1)}, bf16[128,512]{1,0:T(8,128)(2,1)S(1)}, u32[]{:S(2)}, u32[]{:S(2)}) %collective-permute-start.1) | collective-permute-done | bytes 131104 | tf_op jit(solution)/shard_map/ppermute | solution.py:204
  15.6 0.2 transform.5._
  15.8 0.0 copy-start.1
  15.8 0.0 collective-permute-done.piece
  15.8 0.0 copy-done.2
  15.8 0.0 copy-done.3
  15.8 1.1 %convolve.1 = (f32[4,256,512]{2,1,0:T(8,128)S(1)}, bf16[128,256]{1,0:T(8,128)(2,1)S(1)}, bf16[128,256]{1,0:T(8,128)(2,1)S(1)}, bf16[128,256]{1,0:T(8,128)(2,1)S(1)}, bf16[128,256]{1,0:T(8,128)(2,1)S(1)}) custom-call(bf16[128,512]{1,0:T(8,128)(2,1)S(1)} %collective-permute-done.piece, f32[1,4096]{1,0:T(1,128)S(1)} %bitcast.1, ...), custom_call_target="tpu_custom_call", output_to_operand_aliasing={{0}: (4, {})} | custom-call | tf_op jit(solution)/shard_map/convolve/pallas_call | solution.py:159
  16.9 2.0 %collective-permute-start.3 = (bf16[128,256]{1,0:T(8,128)(2,1)S(1)}, bf16[128,256]{1,0:T(8,128)(2,1)S(1)}, u32[]{:S(2)}, u32[]{:S(2)}) collective-permute-start(bf16[128,256]{1,0:T(8,128)(2,1)S(1)} %get-tuple-element.14), channel_id=1, source_target_pairs={{0,8},{8,16},{16,24},{24,0},{1,9},{9,17},{17,25},{25,1},{2,10},{10... | collective-permute-start | bytes 196616 | tf_op jit(solution)/shard_map/ppermute | solution.py:204
  18.8 2.0 %collective-permute-start.4 = (bf16[128,256]{1,0:T(8,128)(2,1)S(1)}, bf16[128,256]{1,0:T(8,128)(2,1)S(1)}, u32[]{:S(2)}, u32[]{:S(2)}) collective-permute-start(bf16[128,256]{1,0:T(8,128)(2,1)S(1)} %get-tuple-element.15), channel_id=1, source_target_pairs={{0,16},{8,24},{16,0},{24,8},{1,17},{9,25},{17,1},{25,9},{2,18},{10... | collective-permute-start | bytes 196616 | tf_op jit(solution)/shard_map/ppermute | solution.py:204
  20.8 2.8 %collective-permute-start.5 = (bf16[128,256]{1,0:T(8,128)(2,1)S(1)}, bf16[128,256]{1,0:T(8,128)(2,1)S(1)}, u32[]{:S(2)}, u32[]{:S(2)}) collective-permute-start(bf16[128,256]{1,0:T(8,128)(2,1)S(1)} %get-tuple-element.16), channel_id=1, source_target_pairs={{0,24},{8,0},{16,8},{24,16},{1,25},{9,1},{17,9},{25,17},{2,26},{10... | collective-permute-start | bytes 196616 | tf_op jit(solution)/shard_map/ppermute | solution.py:204
  23.7 0.0 collective-permute-done.3.refs_1_
  23.7 1.9 %collective-permute-done.4.refs_2_ = bf16[128,256]{1,0:T(8,128)(2,1)S(1)} collective-permute-done((bf16[128,256]{1,0:T(8,128)(2,1)S(1)}, bf16[128,256]{1,0:T(8,128)(2,1)S(1)}, u32[]{:S(2)}, u32[]{:S(2)}) %collective-permute-start.4) | collective-permute-done | bytes 65568 | tf_op jit(solution)/shard_map/ppermute | solution.py:204
  25.6 0.0 collective-permute-done.5.refs_3_
  25.6 0.0 copy-done.1
  25.6 0.8 %gate.1 = bf16[128,1024]{1,0:T(8,128)(2,1)} custom-call(bf16[128,256]{1,0:T(8,128)(2,1)S(1)} %get-tuple-element.13.refs_0_, bf16[128,256]{1,0:T(8,128)(2,1)S(1)} %collective-permute-done.3.refs_1_, bf16[128,256]{1,0:T(8,128)(2,1)S(1)} %collective-permute-done.4.refs_2_, bf16[128,256]{1,0:T(8,128)(2,1)S(1)} %collective-permute-done.5.refs_3_, ...), custom_call_target="tpu_custom_call" | custom-call | tf_op jit(solution)/shard_map/gate/pallas_call | solution.py:189
  (4 shorter events, 0.0 us)
Async XLA Ops:
  0.0 7.8 %copy-start = (bf16[256,256]{1,0:T(8,128)(2,1)S(1)}, bf16[256,256]{1,0:T(8,128)(2,1)}, u32[]{:S(2)}) copy-start(bf16[256,256]{1,0:T(8,128)(2,1)} %constant.27.clone.refs_1_.forward) | copy-start | bytes 393220
  0.9 11.9 %collective-permute-start.2 = (bf16[128,512]{1,0:T(8,128)(2,1)S(1)}, bf16[128,512]{1,0:T(8,128)(2,1)S(1)}, u32[]{:S(2)}, u32[]{:S(2)}) collective-permute-start(bf16[128,512]{1,0:T(8,128)(2,1)S(1)} %pad_maximum_fusion.2), channel_id=1, source_target_pairs={{0,16},{8,24},{16,0},{24,8},{1,17},{9,25},{17,1},{25,9},{2,18},{10... | collective-permute-start | bytes 393224 | tf_op jit(solution)/shard_map/ppermute | solution.py:204
  6.1 9.5 %collective-permute-start.1 = (bf16[128,512]{1,0:T(8,128)(2,1)S(1)}, bf16[128,512]{1,0:T(8,128)(2,1)S(1)}, u32[]{:S(2)}, u32[]{:S(2)}) collective-permute-start(bf16[128,512]{1,0:T(8,128)(2,1)S(1)} %pad_maximum_fusion.1), channel_id=1, source_target_pairs={{0,8},{8,0},{16,24},{24,16},{1,9},{9,1},{17,25},{25,17},{2,10},{10... | collective-permute-start | bytes 393224 | tf_op jit(solution)/shard_map/ppermute | solution.py:204
  7.7 8.1 %collective-permute-start = (bf16[128,512]{1,0:T(8,128)(2,1)S(1)}, bf16[128,512]{1,0:T(8,128)(2,1)S(1)}, u32[]{:S(2)}, u32[]{:S(2)}) collective-permute-start(bf16[128,512]{1,0:T(8,128)(2,1)S(1)} %pad_maximum_fusion), channel_id=1, source_target_pairs={{0,24},{8,16},{16,8},{24,0},{1,25},{9,17},{17,9},{25,1},{2,26},{10... | collective-permute-start | bytes 393224 | tf_op jit(solution)/shard_map/ppermute | solution.py:204
  13.0 2.8 %copy-start.2 = (bf16[128,768]{1,0:T(8,128)(2,1)S(1)}, bf16[128,768]{1,0:T(8,128)(2,1)}, u32[]{:S(2)}) copy-start(bf16[128,768]{1,0:T(8,128)(2,1)} %constant.28.clone.back) | copy-start | bytes 589828
  13.0 2.8 %copy-start.3 = (f32[4096]{0:T(1024)S(1)}, f32[4096]{0:T(1024)}, u32[]{:S(2)}) copy-start(f32[4096]{0:T(1024)} %param.8) | copy-start | bytes 49156
  15.8 9.8 %copy-start.1 = (bf16[128,1024]{1,0:T(8,128)(2,1)S(1)}, bf16[128,1024]{1,0:T(8,128)(2,1)}, u32[]{:S(2)}) copy-start(bf16[128,1024]{1,0:T(8,128)(2,1)} %refs_4_.1) | copy-start | bytes 786436
  16.9 6.8 %collective-permute-start.3 = (bf16[128,256]{1,0:T(8,128)(2,1)S(1)}, bf16[128,256]{1,0:T(8,128)(2,1)S(1)}, u32[]{:S(2)}, u32[]{:S(2)}) collective-permute-start(bf16[128,256]{1,0:T(8,128)(2,1)S(1)} %get-tuple-element.14), channel_id=1, source_target_pairs={{0,8},{8,16},{16,24},{24,0},{1,9},{9,17},{17,25},{25,1},{2,10},{10... | collective-permute-start | bytes 196616 | tf_op jit(solution)/shard_map/ppermute | solution.py:204
  18.8 6.8 %collective-permute-start.4 = (bf16[128,256]{1,0:T(8,128)(2,1)S(1)}, bf16[128,256]{1,0:T(8,128)(2,1)S(1)}, u32[]{:S(2)}, u32[]{:S(2)}) collective-permute-start(bf16[128,256]{1,0:T(8,128)(2,1)S(1)} %get-tuple-element.15), channel_id=1, source_target_pairs={{0,16},{8,24},{16,0},{24,8},{1,17},{9,25},{17,1},{25,9},{2,18},{10... | collective-permute-start | bytes 196616 | tf_op jit(solution)/shard_map/ppermute | solution.py:204
  20.8 4.8 %collective-permute-start.5 = (bf16[128,256]{1,0:T(8,128)(2,1)S(1)}, bf16[128,256]{1,0:T(8,128)(2,1)S(1)}, u32[]{:S(2)}, u32[]{:S(2)}) collective-permute-start(bf16[128,256]{1,0:T(8,128)(2,1)S(1)} %get-tuple-element.16), channel_id=1, source_target_pairs={{0,24},{8,0},{16,8},{24,16},{1,25},{9,1},{17,9},{25,17},{2,26},{10... | collective-permute-start | bytes 196616 | tf_op jit(solution)/shard_map/ppermute | solution.py:204

commit v3 on v2

--- a/solution.py
+++ b/solution.py
@@ -12,8 +12,8 @@
 LANES = 128
 MIB = 1 << 20
 VMEM = pl.BlockSpec(memory_space=pltpu.VMEM)
-OUT = ("swap", 2, 1, 3)
-BACK = ("ring", 1, 2, 3)
+OUT = ("swap", 3, 1, 2)
+BACK = ("ring", 2, 1, 3)
 
 
 def split(table):
@@ -87,13 +87,13 @@
     transform_into(OUT, step, piece, table, spectra)
 
 
-def transform(spectra, step, piece, table, count):
+def transform(spectra, step, piece, table, count, after=()):
     shape = jax.ShapeDtypeStruct((count, table.shape[0], piece.shape[1]), jnp.float32)
     held = [] if spectra is None else [spectra]
     return pl.pallas_call(
         functools.partial(transform_kernel, step),
         out_shape=shape,
-        in_specs=[VMEM] * (2 + len(held)),
+        in_specs=[VMEM] * (2 + len(held) + len(after)),
         out_specs=VMEM,
         input_output_aliases={2: 0} if held else {},
         compiler_params=pltpu.CompilerParams(vmem_limit_bytes=2 * MIB),
@@ -103,18 +103,30 @@
             transcendentals=0,
         ),
         name="transform",
-    )(piece, table, *held)
-
-
-def conv_kernel(count, step, piece, bias, forward, back, _, spectra, *refs):
-    outs, total, result = refs[:count], refs[count], refs[count + 1]
-    rows, lanes = outs[0].shape
-    me = lax.axis_index("ctx")
-    transform_into(OUT, step, piece, forward, spectra)
+    )(piece, table, *held, *after)
+
+
+def bias_base(count, lanes):
+    if lanes % LANES:
+        return 0
+    first = (lax.axis_index("lag") * count + lax.axis_index("ctx")) * lanes
+    return pl.multiple_of(first, LANES)
+
+
+def inverse(y, back):
+    upper = y.astype(jnp.bfloat16)
+    lower = (y - upper.astype(jnp.float32)).astype(jnp.bfloat16)
+    return dot(back[...], jnp.concatenate([upper, upper, lower], 0)).astype(jnp.bfloat16)
+
+
+def products(spectra, bias, sums, total, ready, wanted, closes):
+    count, length, both = spectra.shape
+    rows, lanes = length // 2, both // 2
     width = min(lanes, LANES)
-    base = 0
-    if lanes % LANES == 0:
-        base = pl.multiple_of((lax.axis_index("lag") * count + me) * lanes, LANES)
+    base = bias_base(count, lanes)
+    meets = [[i for i in range(r + 1) if wanted(i, r - i)] for r in range(count)]
+    values = sorted({i for r in range(count) for i in meets[r]})
+    taps = sorted({r - i for r in range(count) for i in meets[r]})
 
     def tile(t, sign):
         re = pl.ds(pl.multiple_of(t * 8, 8), 8)
@@ -122,20 +134,28 @@
         for first in range(0, lanes, width):
             val = slice(first, first + width)
             tap = slice(lanes + first, lanes + first + width)
-            val_re = [spectra[i, re, val] for i in range(count)]
-            val_im = [spectra[i, im, val] for i in range(count)]
-            tap_re = [spectra[i, re, tap] for i in range(count)]
-            tap_im = [spectra[i, im, tap] for i in range(count)]
-            tap_re[0] = tap_re[0] + bias[:, pl.ds(base + first, width)]
-            last_re = last_im = 0.0
+            val_re = {i: spectra[i, re, val] for i in values}
+            val_im = {i: spectra[i, im, val] for i in values}
+            tap_re = {j: spectra[j, re, tap] for j in taps}
+            tap_im = {j: spectra[j, im, tap] for j in taps}
+            if 0 in taps:
+                tap_re[0] = tap_re[0] + bias[:, pl.ds(base + first, width)]
+            last_re = last_im = None
             for r in range(count):
-                sum_re = sum_im = 0.0
-                for i in range(r + 1):
+                sum_re = sum_im = None
+                if r in ready:
+                    sum_re, sum_im = sums[r, re, val], sums[r, im, val]
+                for i in meets[r]:
                     a, b, c, d = val_re[i], val_im[i], tap_re[r - i], tap_im[r - i]
-                    sum_re = sum_re + (a * c - b * d)
-                    sum_im = sum_im + (a * d + b * c)
-                total[r, re, val] = sum_re - sign * last_im
-                total[r, im, val] = sum_im + sign * last_re
+                    new_re, new_im = a * c - b * d, a * d + b * c
+                    sum_re = new_re if sum_re is None else sum_re + new_re
+                    sum_im = new_im if sum_im is None else sum_im + new_im
+                if closes(r):
+                    total[r, re, val] = sum_re if r == 0 else sum_re - sign * last_im
+                    total[r, im, val] = sum_im if r == 0 else sum_im + sign * last_re
+                if sums is not None and meets[r] and r not in ready:
+                    sums[r, re, val] = sum_re
+                    sums[r, im, val] = sum_im
                 last_re, last_im = sum_re, sum_im
 
     half = rows // 16
@@ -143,57 +163,187 @@
     pl.loop(0, half, unroll=unroll)(lambda t: tile(t, 1.0))
     pl.loop(half, 2 * half, unroll=unroll)(lambda t: tile(t, -1.0))
 
+
+def early_kernel(count, last, bias, back, spectra, sums, early, total):
+    missing = came(OUT, count, lax.axis_index("ctx"), last)
+    for m in range(count):
+
+        @pl.when(missing == m)
+        def _(m=m):
+            products(
+                spectra, bias, sums, total, (), lambda i, j: m not in (i, j), lambda r: r < m
+            )
+            for r in range(m):
+                early[r] = inverse(total[r], back)
+
+
+def late_kernel(count, last, piece, bias, forward, back, sums, early, _, spectra, *refs):
+    outs, total, result = refs[:count], refs[count], refs[count + 1]
+    me = lax.axis_index("ctx")
+    missing = came(OUT, count, me, last)
+    transform_into(OUT, last, piece, forward, spectra)
+    for m in range(count):
+
+        @pl.when(missing == m)
+        def _(m=m):
+            ready = [r for r in range(count) if any(m not in (i, r - i) for i in range(r + 1))]
+            products(
+                spectra, bias, sums, total, ready, lambda i, j: m in (i, j), lambda r: r >= m
+            )
+            for r in range(count):
+                result[r] = early[r] if r < m else inverse(total[r], back)
+
+    for place, step in enumerate([0] + steps(BACK, count)):
+        outs[place][...] = result[to(BACK, count, me, step)]
+
+
+def whole_kernel(count, last, piece, bias, forward, back, _, spectra, *refs):
+    outs, total, result = refs[:count], refs[count], refs[count + 1]
+    me = lax.axis_index("ctx")
+    transform_into(OUT, last, piece, forward, spectra)
+    products(spectra, bias, None, total, (), lambda i, j: True, lambda r: True)
     for r in range(count):
-        y = total[r]
-        upper = y.astype(jnp.bfloat16)
-        lower = (y - upper.astype(jnp.float32)).astype(jnp.bfloat16)
-        conv = dot(back[...], jnp.concatenate([upper, upper, lower], 0))
-        result[r] = conv.astype(jnp.bfloat16)
-    for place, step_back in enumerate([0] + steps(BACK, count)):
-        outs[place][...] = result[to(BACK, count, me, step_back)]
-
-
-def convolve(spectra, step, piece, bias, forward, back):
+        result[r] = inverse(total[r], back)
+    for place, step in enumerate([0] + steps(BACK, count)):
+        outs[place][...] = result[to(BACK, count, me, step)]
+
+
+def convolve(spectra, last, piece, bias, forward, back):
     count, length, both = spectra.shape
     rows, lanes = length // 2, both // 2
-    outs = pl.pallas_call(
-        functools.partial(conv_kernel, count, step),
+    totals = jax.ShapeDtypeStruct((count, length, lanes), jnp.float32)
+    results = jax.ShapeDtypeStruct((count, rows, lanes), jnp.bfloat16)
+    held = []
+    if count <= 4:
+        held = pl.pallas_call(
+            functools.partial(early_kernel, count, last),
+            out_shape=[totals, results],
+            in_specs=[VMEM] * 3,
+            out_specs=[VMEM] * 2,
+            scratch_shapes=[pltpu.VMEM(totals.shape, totals.dtype)],
+            compiler_params=pltpu.CompilerParams(vmem_limit_bytes=4 * MIB),
+            cost_estimate=pl.CostEstimate(
+                flops=3 * 2 * back.size * lanes, bytes_accessed=4 * spectra.size, transcendentals=0
+            ),
+            name="early_products",
+        )(bias, back, spectra)
+    return pl.pallas_call(
+        functools.partial(late_kernel if held else whole_kernel, count, last),
         out_shape=[jax.ShapeDtypeStruct(spectra.shape, jnp.float32)]
         + [jax.ShapeDtypeStruct((rows, lanes), jnp.bfloat16)] * count,
-        in_specs=[VMEM] * 5,
+        in_specs=[VMEM] * (5 + len(held)),
         out_specs=[VMEM] * (count + 1),
         scratch_shapes=[
-            pltpu.VMEM((count, length, lanes), jnp.float32),
-            pltpu.VMEM((count, rows, lanes), jnp.bfloat16),
+            pltpu.VMEM(totals.shape, totals.dtype),
+            pltpu.VMEM(results.shape, results.dtype),
         ],
-        input_output_aliases={4: 0},
+        input_output_aliases={4 + len(held): 0},
         compiler_params=pltpu.CompilerParams(vmem_limit_bytes=8 * MIB),
         name="convolve",
-    )(piece, bias, forward, back, spectra)
-    return outs[1:]
-
-
-def gate_kernel(count, lanes, *refs):
-    pieces, gate, out = refs[:count], refs[count], refs[count + 1]
-    me = lax.axis_index("ctx")
-    for place, step in enumerate([0] + steps(BACK, count)):
-        cols = pl.ds(pl.multiple_of(came(BACK, count, me, step) * lanes, LANES), lanes)
-        mixed = gate[:, cols].astype(jnp.float32) * pieces[place][...].astype(jnp.float32)
-        out[:, cols] = mixed.astype(jnp.bfloat16)
+    )(piece, bias, forward, back, *held, spectra)[1:]
+
+
+def gated(gate, cols, piece):
+    return (gate[:, cols].astype(jnp.float32) * piece.astype(jnp.float32)).astype(jnp.bfloat16)
+
+
+def first_block_kernel(count, lanes, *refs):
+    pieces = refs[: count - 1]
+    bias, forward, back, gate, out, token, spectrum, total, mixed, sem = refs[count - 1 :]
+    rows = out.shape[0]
+    lag = lax.axis_index("lag")
+    token[...] = jnp.zeros_like(token)
+
+    @pl.when(lax.axis_index("ctx") == 0)
+    def _():
+        for step, piece in zip(steps(OUT, count), pieces):
+            owner = step
+            cols = slice(owner * lanes, (owner + 1) * lanes)
+            x = piece[...]
+            spectrum[...] = dot(forward[...], jnp.concatenate([x, x], 0))
+            start = pl.multiple_of((lag * count + owner) * lanes, LANES)
+            a, b = spectrum[:rows, :lanes], spectrum[rows:, :lanes]
+            c = spectrum[:rows, lanes:] + bias[:, pl.ds(start, lanes)]
+            d = spectrum[rows:, lanes:]
+            total[:rows] = a * c - b * d
+            total[rows:] = a * d + b * c
+            mixed[:, cols] = gated(gate, cols, inverse(total[...], back))
+        copy = pltpu.make_async_copy(mixed.at[:, lanes:], out.at[:, lanes:], sem)
+        copy.start()
+        copy.wait()
+
+
+def first_block(pieces, bias, forward, back, gate):
+    count = len(pieces) + 1
+    lanes = pieces[0].shape[1] // 2
+    length = forward.shape[0]
+    return pl.pallas_call(
+        functools.partial(first_block_kernel, count, lanes),
+        out_shape=[
+            jax.ShapeDtypeStruct(gate.shape, jnp.bfloat16),
+            jax.ShapeDtypeStruct((8, LANES), jnp.float32),
+        ],
+        in_specs=[VMEM] * (count + 3),
+        out_specs=[pl.BlockSpec(memory_space=pltpu.HBM), VMEM],
+        scratch_shapes=[
+            pltpu.VMEM((length, 2 * lanes), jnp.float32),
+            pltpu.VMEM((length, lanes), jnp.float32),
+            pltpu.VMEM(gate.shape, jnp.bfloat16),
+            pltpu.SemaphoreType.DMA,
+        ],
+        compiler_params=pltpu.CompilerParams(vmem_limit_bytes=4 * MIB),
+        cost_estimate=pl.CostEstimate(
+            flops=2 * (count - 1) * forward.size * 2 * lanes, bytes_accessed=0, transcendentals=0
+        ),
+        name="first_block",
+    )(*pieces, bias, forward, back, gate)
+
+
+def put_kernel(places, count, *refs):
+    pieces, gate, out, mixed, sems = refs[: len(places)], refs[-5], refs[-3], refs[-2], refs[-1]
+    lanes = pieces[0].shape[1]
+    me = lax.axis_index("ctx")
+    order = [0] + steps(BACK, count)
+
+    def put(todo):
+        copies = []
+        for k in todo:
+            owner = came(BACK, count, me, order[places[k]])
+            cols = pl.ds(pl.multiple_of(owner * lanes, LANES), lanes)
+            mixed[k] = gated(gate, cols, pieces[k][...])
+            copies.append(pltpu.make_async_copy(mixed.at[k], out.at[:, cols], sems.at[k]))
+            copies[-1].start()
+        for copy in copies:
+            copy.wait()
+
+    mine = [k for k, place in enumerate(places) if place == 0]
+    if mine:
+        put(mine)
+
+    @pl.when(me != 0)
+    def _():
+        put([k for k in range(len(places)) if k not in mine])
+
+
+def put(places, pieces, gate, out):
+    count = gate.shape[1] // pieces[0].shape[1]
+    hbm = pl.BlockSpec(memory_space=pltpu.HBM)
+    return pl.pallas_call(
+        functools.partial(put_kernel, places, count),
+        out_shape=jax.ShapeDtypeStruct(gate.shape, jnp.bfloat16),
+        in_specs=[VMEM] * (len(pieces) + 1) + [hbm],
+        out_specs=hbm,
+        scratch_shapes=[
+            pltpu.VMEM((len(places),) + pieces[0].shape, jnp.bfloat16),
+            pltpu.SemaphoreType.DMA((len(places),)),
+        ],
+        input_output_aliases={len(pieces) + 1: 0},
+        compiler_params=pltpu.CompilerParams(vmem_limit_bytes=MIB),
+        name="put",
+    )(*pieces, gate, out)
 
 
 def apply_gate(returned, gate):
-    count = len(returned)
-    lanes = returned[0].shape[1]
-    if lanes % LANES == 0:
-        return pl.pallas_call(
-            functools.partial(gate_kernel, count, lanes),
-            out_shape=jax.ShapeDtypeStruct(gate.shape, jnp.bfloat16),
-            in_specs=[VMEM] * (count + 1),
-            out_specs=VMEM,
-            compiler_params=pltpu.CompilerParams(vmem_limit_bytes=2 * MIB),
-            name="gate",
-        )(*returned, gate)
     me = lax.axis_index("ctx")
     ordered = jnp.roll(jnp.stack(returned)[::-1], me + 1, 0)
     whole = jnp.transpose(ordered, (1, 0, 2)).reshape(gate.shape)
@@ -217,11 +367,18 @@
     out_steps, back_steps = steps(OUT, count), steps(BACK, count)
     arrived = [move(OUT, count, step, piece) for step, piece in zip(out_steps, pieces)]
     spectra = transform(None, 0, own, forward, count)
+    after = []
+    if lanes % LANES == 0:
+        out, *after = first_block(pieces, own_bias, forward, back, gate)
     for step, piece in zip(out_steps[:-1], arrived):
-        spectra = transform(spectra, step, piece, forward, count)
+        spectra = transform(spectra, step, piece, forward, count, after)
+        after = []
     done = convolve(spectra, out_steps[-1], arrived[-1], own_bias, forward, back)
     returned = [move(BACK, count, step, piece) for step, piece in zip(back_steps, done[1:])]
-    return apply_gate([done[0]] + returned, gate)
+    if lanes % LANES:
+        return apply_gate([done[0]] + returned, gate)
+    out = put((0,), done[:1], gate, out)
+    return put(tuple(range(1, count)), returned, gate, out)
 
 
 def solution(mesh):

time: 26.6 us -> 25.9 us (0.974)
  starting transfers between devices: 12.6 us -> 10.2 us
  Pallas kernels: 2.48 us -> 4.16 us
    ppermute x6, starting transfers between devices: 12.6 us -> 10.2 us  [move(): return lax.ppermute(piece, 'ctx', pairs(plan, count, step))]
    pallas_call x2 -> x5, Pallas kernels: 1.83 us -> 3.49 us  [the longest x1 1.64 us: first_block(): pl.pallas_call(functools.partial(first_block_kernel, count, lanes), out_s...]
  transfers between devices with their start and end apart: 6 -> 6, of which waited for: 3 -> 5; matrix products, arithmetic and copies ran while one was open for 4% -> 4% of each run, Pallas kernels for 2% -> 13%
where the time goes in v3:
time: 25.9 us; the launch traced here: 25.7 us
  starting transfers between devices  10.2 us (39%)
  waiting for transfers between devices  9.21 us (36%)
  Pallas kernels  4.16 us (16%)
  local copies, waits for them, and re-layouts  1.97 us (8%)
    ppermute x6, starting transfers between devices, move(): return lax.ppermute(piece, 'ctx', pairs(plan, count, step))  10.2 us
    ppermute x6, waiting for transfers between devices, move(): return lax.ppermute(piece, 'ctx', pairs(plan, count, step))  9.21 us
    dynamic_slice x2, local copies, waits for them, and re-layouts, piece(): lax.dynamic_slice_in_dim(array, start, lanes, 1)  1.95 us
    pallas_call x1, Pallas kernels, first_block(): pl.pallas_call(functools.partial(first_block_kernel, count, lanes), out_s...  1.64 us
    pallas_call x1, Pallas kernels, convolve(): pl.pallas_call(functools.partial(late_kernel if held else whole_kernel, c...  0.69 us
    pallas_call x2, Pallas kernels, put(): pl.pallas_call(functools.partial(put_kernel, places, count), out_shape=ja...  0.68 us
    pallas_call x3, Pallas kernels, transform(): pl.pallas_call(functools.partial(transform_kernel, step), out_shape=shape...  0.66 us
  transfers between devices with their start and end apart: 6, of which 5 were waited for; matrix products, arithmetic and copies ran while one was open for 4% of the time, Pallas kernels for 13%

profile of v3, /device:TPU:0, one launch (start us, length us, event | category | flops | bytes accessed | tf_op | source)
XLA Modules:
  0.0 25.7 jit_solution(10713411580314679522)
XLA Ops:
  0.0 0.0 copy-start
  0.0 0.9 %constant_dynamic-slice_fusion.2 = (bf16[128,256]{1,0:T(8,128)(2,1)S(1)}, bf16[128,256]{1,0:T(8,128)(2,1)S(1)}) fusion(bf16[128,4096]{1,0:T(8,128)(2,1)} %param.9, s32[]{:T(128)S(6)} %select_n.18, bf16[128,4096]{1,0:T(8,128)(2,1)} %param.6), kind=kLoop, calls=%fused_computation.6 | loop fusion | bytes 262148 | tf_op jit(solution)/shard_map/dynamic_slice | solution.py:70
  0.9 0.0 copy-start.1
  0.9 0.0 copy-start.2
  0.9 0.0 copy-start.3
  1.0 5.1 %collective-permute-start.2 = (bf16[128,512]{1,0:T(8,128)(2,1)S(1)}, bf16[128,512]{1,0:T(8,128)(2,1)S(1)}, u32[]{:S(2)}, u32[]{:S(2)}) collective-permute-start(bf16[128,512]{1,0:T(8,128)(2,1)S(1)} %pad_maximum_fusion.2.refs_0_), channel_id=1, source_target_pairs={{0,24},{8,16},{16,8},{24,0},{1,25},{9,17},{17,9},{25,1},{2,26},{10... | collective-permute-start | bytes 393224 | tf_op jit(solution)/shard_map/ppermute | solution.py:354
  6.1 1.0 %constant_dynamic-slice_fusion = (bf16[128,256]{1,0:T(8,128)(2,1)S(1)}, bf16[128,256]{1,0:T(8,128)(2,1)S(1)}, bf16[128,256]{1,0:T(8,128)(2,1)S(1)}, bf16[128,256...) fusion(bf16[128,4096]{1,0:T(8,128)(2,1)} %param.9, s32[]{:T(128)S(6)} %select_n.19, ...), kind=kLoop, calls=%fused_computation.4 | loop fusion | bytes 786444 | tf_op jit(solution)/shard_map/dynamic_slice | solution.py:70
  7.1 0.1 collective-permute-start
  7.2 0.7 %collective-permute-start.1 = (bf16[128,512]{1,0:T(8,128)(2,1)S(1)}, bf16[128,512]{1,0:T(8,128)(2,1)S(1)}, u32[]{:S(2)}, u32[]{:S(2)}) collective-permute-start(bf16[128,512]{1,0:T(8,128)(2,1)S(1)} %pad_maximum_fusion.1.refs_1_), channel_id=1, source_target_pairs={{0,8},{8,0},{16,24},{24,16},{1,9},{9,1},{17,25},{25,17},{2,10},{10... | collective-permute-start | bytes 393224 | tf_op jit(solution)/shard_map/ppermute | solution.py:354
  7.9 0.0 copy-done
  7.9 0.2 transform.3.refs_2_
  8.2 0.0 copy-done.1
  8.2 0.0 copy-done.2
  8.2 0.0 copy-done.3
  8.2 1.6 %first_block.1 = (bf16[128,1024]{1,0:T(8,128)(2,1)}, f32[8,128]{1,0:T(8,128)S(1)}) custom-call(bf16[128,512]{1,0:T(8,128)(2,1)S(1)} %pad_maximum_fusion.2.refs_0_, bf16[128,512]{1,0:T(8,128)(2,1)S(1)} %pad_maximum_fusion.1.refs_1_, bf16[128,512]{1,0:T(8,128)(2,1)S(1)} %pad_maximum_fusion.refs_2_, f32[1,4096]{1,0:T(1,128)S(1)} %bitcast.1, ...), custom_call_target="tpu_custom_call" | custom-call | flops 201326592 | tf_op jit(solution)/shard_map/first_block/pallas_call | solution.py:280
  9.8 0.2 collective-permute-done.2.refs_0_
  10.0 0.2 transform.4.refs_2_
  10.2 4.3 %collective-permute-done.1.refs_0_ = bf16[128,512]{1,0:T(8,128)(2,1)S(1)} collective-permute-done((bf16[128,512]{1,0:T(8,128)(2,1)S(1)}, bf16[128,512]{1,0:T(8,128)(2,1)S(1)}, u32[]{:S(2)}, u32[]{:S(2)}) %collective-permute-start.1) | collective-permute-done | bytes 131104 | tf_op jit(solution)/shard_map/ppermute | solution.py:354
  14.5 0.2 transform.5.spectra._
  14.7 0.5 %early_products.1 = (f32[4,256,256]{2,1,0:T(8,128)S(1)}, bf16[4,128,256]{2,1,0:T(8,128)(2,1)S(1)}) custom-call(f32[1,4096]{1,0:T(1,128)S(1)} %bitcast.2, bf16[128,768]{1,0:T(8,128)(2,1)S(1)} %copy-done.2, f32[4,256,512]{2,1,0:T(8,128)S(1)} %transform.5.spectra._), custom_call_target="tpu_custom_call" | custom-call | flops 150994944 | bytes 2097152 | tf_op jit(solution)/shard_map/early_products/pallas_call | solution.py:218
  15.2 1.9 %collective-permute-done.piece = bf16[128,512]{1,0:T(8,128)(2,1)S(1)} collective-permute-done((bf16[128,512]{1,0:T(8,128)(2,1)S(1)}, bf16[128,512]{1,0:T(8,128)(2,1)S(1)}, u32[]{:S(2)}, u32[]{:S(2)}) %collective-permute-start) | collective-permute-done | bytes 131104 | tf_op jit(solution)/shard_map/ppermute | solution.py:354
  17.2 0.7 %convolve.1 = (f32[4,256,512]{2,1,0:T(8,128)S(1)}, bf16[128,256]{1,0:T(8,128)(2,1)S(1)}, bf16[128,256]{1,0:T(8,128)(2,1)S(1)}, bf16[128,256]{1,0:T(8,128)(2,1)S(1)}, bf16[128,256]{1,0:T(8,128)(2,1)S(1)}) custom-call(bf16[128,512]{1,0:T(8,128)(2,1)S(1)} %collective-permute-done.piece, f32[1,4096]{1,0:T(1,128)S(1)} %bitcast.3, ...), custom_call_target="tpu_custom_call", output_to_operand_aliasing={{0}: (6, {})} | custom-call | tf_op jit(solution)/shard_map/convolve/pallas_call | solution.py:230
  17.9 0.5 %collective-permute-start.3 = (bf16[128,256]{1,0:T(8,128)(2,1)S(1)}, bf16[128,256]{1,0:T(8,128)(2,1)S(1)}, u32[]{:S(2)}, u32[]{:S(2)}) collective-permute-start(bf16[128,256]{1,0:T(8,128)(2,1)S(1)} %get-tuple-element.20), channel_id=1, source_target_pairs={{0,16},{8,24},{16,0},{24,8},{1,17},{9,25},{17,1},{25,9},{2,18},{10... | collective-permute-start | bytes 196616 | tf_op jit(solution)/shard_map/ppermute | solution.py:354
  18.3 2.8 %collective-permute-start.4 = (bf16[128,256]{1,0:T(8,128)(2,1)S(1)}, bf16[128,256]{1,0:T(8,128)(2,1)S(1)}, u32[]{:S(2)}, u32[]{:S(2)}) collective-permute-start(bf16[128,256]{1,0:T(8,128)(2,1)S(1)} %get-tuple-element.21), channel_id=1, source_target_pairs={{0,8},{8,16},{16,24},{24,0},{1,9},{9,17},{17,25},{25,1},{2,10},{10... | collective-permute-start | bytes 196616 | tf_op jit(solution)/shard_map/ppermute | solution.py:354
  21.1 1.1 %collective-permute-start.5 = (bf16[128,256]{1,0:T(8,128)(2,1)S(1)}, bf16[128,256]{1,0:T(8,128)(2,1)S(1)}, u32[]{:S(2)}, u32[]{:S(2)}) collective-permute-start(bf16[128,256]{1,0:T(8,128)(2,1)S(1)} %get-tuple-element.22), channel_id=1, source_target_pairs={{0,24},{8,0},{16,8},{24,16},{1,25},{9,1},{17,9},{25,17},{2,26},{10... | collective-permute-start | bytes 196616 | tf_op jit(solution)/shard_map/ppermute | solution.py:354
  22.2 0.7 %put.2.refs_4_ = bf16[128,1024]{1,0:T(8,128)(2,1)} custom-call(bf16[128,256]{1,0:T(8,128)(2,1)S(1)} %get-tuple-element.23.refs_0_, bf16[128,1024]{1,0:T(8,128)(2,1)S(1)} %copy-done.1, bf16[128,1024]{1,0:T(8,128)(2,1)} %get-tuple-element.24.refs_2_), custom_call_target="tpu_custom_call", output_to_operand_aliasing={{}: (2, {})} | custom-call | tf_op jit(solution)/shard_map/put/pallas_call | solution.py:331
  22.8 2.4 %collective-permute-done.3.refs_0_ = bf16[128,256]{1,0:T(8,128)(2,1)S(1)} collective-permute-done((bf16[128,256]{1,0:T(8,128)(2,1)S(1)}, bf16[128,256]{1,0:T(8,128)(2,1)S(1)}, u32[]{:S(2)}, u32[]{:S(2)}) %collective-permute-start.3) | collective-permute-done | bytes 65568 | tf_op jit(solution)/shard_map/ppermute | solution.py:354
  25.3 0.0 collective-permute-done.4.refs_1_
  25.3 0.4 %collective-permute-done.5.refs_2_ = bf16[128,256]{1,0:T(8,128)(2,1)S(1)} collective-permute-done((bf16[128,256]{1,0:T(8,128)(2,1)S(1)}, bf16[128,256]{1,0:T(8,128)(2,1)S(1)}, u32[]{:S(2)}, u32[]{:S(2)}) %collective-permute-start.5) | collective-permute-done | bytes 65568 | tf_op jit(solution)/shard_map/ppermute | solution.py:354
  (5 shorter events, 0.1 us)
Async XLA Ops:
  0.0 7.9 %copy-start = (bf16[256,256]{1,0:T(8,128)(2,1)S(1)}, bf16[256,256]{1,0:T(8,128)(2,1)}, u32[]{:S(2)}) copy-start(bf16[256,256]{1,0:T(8,128)(2,1)} %constant.27.clone.refs_1_.refs_4_.forward) | copy-start | bytes 393220
  0.9 7.2 %copy-start.1 = (bf16[128,1024]{1,0:T(8,128)(2,1)S(1)}, bf16[128,1024]{1,0:T(8,128)(2,1)}, u32[]{:S(2)}) copy-start(bf16[128,1024]{1,0:T(8,128)(2,1)} %refs_3_.1) | copy-start | bytes 786436
  0.9 7.2 %copy-start.2 = (bf16[128,768]{1,0:T(8,128)(2,1)S(1)}, bf16[128,768]{1,0:T(8,128)(2,1)}, u32[]{:S(2)}) copy-start(bf16[128,768]{1,0:T(8,128)(2,1)} %constant.28.clone.refs_5_.back) | copy-start | bytes 589828
  0.9 7.2 %copy-start.3 = (f32[4096]{0:T(1024)S(1)}, f32[4096]{0:T(1024)}, u32[]{:S(2)}) copy-start(f32[4096]{0:T(1024)} %param.8) | copy-start | bytes 49156
  1.0 9.0 %collective-permute-start.2 = (bf16[128,512]{1,0:T(8,128)(2,1)S(1)}, bf16[128,512]{1,0:T(8,128)(2,1)S(1)}, u32[]{:S(2)}, u32[]{:S(2)}) collective-permute-start(bf16[128,512]{1,0:T(8,128)(2,1)S(1)} %pad_maximum_fusion.2.refs_0_), channel_id=1, source_target_pairs={{0,24},{8,16},{16,8},{24,0},{1,25},{9,17},{17,9},{25,1},{2,26},{10... | collective-permute-start | bytes 393224 | tf_op jit(solution)/shard_map/ppermute | solution.py:354
  7.1 10.0 %collective-permute-start = (bf16[128,512]{1,0:T(8,128)(2,1)S(1)}, bf16[128,512]{1,0:T(8,128)(2,1)S(1)}, u32[]{:S(2)}, u32[]{:S(2)}) collective-permute-start(bf16[128,512]{1,0:T(8,128)(2,1)S(1)} %pad_maximum_fusion.refs_2_), channel_id=1, source_target_pairs={{0,16},{8,24},{16,0},{24,8},{1,17},{9,25},{17,1},{25,9},{2,18},{10... | collective-permute-start | bytes 393224 | tf_op jit(solution)/shard_map/ppermute | solution.py:354
  7.2 7.3 %collective-permute-start.1 = (bf16[128,512]{1,0:T(8,128)(2,1)S(1)}, bf16[128,512]{1,0:T(8,128)(2,1)S(1)}, u32[]{:S(2)}, u32[]{:S(2)}) collective-permute-start(bf16[128,512]{1,0:T(8,128)(2,1)S(1)} %pad_maximum_fusion.1.refs_1_), channel_id=1, source_target_pairs={{0,8},{8,0},{16,24},{24,16},{1,9},{9,1},{17,25},{25,17},{2,10},{10... | collective-permute-start | bytes 393224 | tf_op jit(solution)/shard_map/ppermute | solution.py:354
  17.9 7.4 %collective-permute-start.3 = (bf16[128,256]{1,0:T(8,128)(2,1)S(1)}, bf16[128,256]{1,0:T(8,128)(2,1)S(1)}, u32[]{:S(2)}, u32[]{:S(2)}) collective-permute-start(bf16[128,256]{1,0:T(8,128)(2,1)S(1)} %get-tuple-element.20), channel_id=1, source_target_pairs={{0,16},{8,24},{16,0},{24,8},{1,17},{9,25},{17,1},{25,9},{2,18},{10... | collective-permute-start | bytes 196616 | tf_op jit(solution)/shard_map/ppermute | solution.py:354
  18.3 6.9 %collective-permute-start.4 = (bf16[128,256]{1,0:T(8,128)(2,1)S(1)}, bf16[128,256]{1,0:T(8,128)(2,1)S(1)}, u32[]{:S(2)}, u32[]{:S(2)}) collective-permute-start(bf16[128,256]{1,0:T(8,128)(2,1)S(1)} %get-tuple-element.21), channel_id=1, source_target_pairs={{0,8},{8,16},{16,24},{24,0},{1,9},{9,17},{17,25},{25,1},{2,10},{10... | collective-permute-start | bytes 196616 | tf_op jit(solution)/shard_map/ppermute | solution.py:354
  21.1 4.6 %collective-permute-start.5 = (bf16[128,256]{1,0:T(8,128)(2,1)S(1)}, bf16[128,256]{1,0:T(8,128)(2,1)S(1)}, u32[]{:S(2)}, u32[]{:S(2)}) collective-permute-start(bf16[128,256]{1,0:T(8,128)(2,1)S(1)} %get-tuple-element.22), channel_id=1, source_target_pairs={{0,24},{8,0},{16,8},{24,16},{1,25},{9,1},{17,9},{25,17},{2,26},{10... | collective-permute-start | bytes 196616 | tf_op jit(solution)/shard_map/ppermute | solution.py:354

commit v4 on v3

--- a/solution.py
+++ b/solution.py
@@ -84,6 +84,8 @@
 
 def transform_kernel(step, *refs):
     piece, table, spectra = refs[0], refs[1], refs[-1]
+    if step:
+        spectra[...] = refs[2][...]
     transform_into(OUT, step, piece, table, spectra)
 
 
@@ -119,8 +121,8 @@
     return dot(back[...], jnp.concatenate([upper, upper, lower], 0)).astype(jnp.bfloat16)
 
 
-def products(spectra, bias, sums, total, ready, wanted, closes):
-    count, length, both = spectra.shape
+def products(at, shape, bias, sums, total, ready, wanted, closes):
+    count, length, both = shape
     rows, lanes = length // 2, both // 2
     width = min(lanes, LANES)
     base = bias_base(count, lanes)
@@ -134,10 +136,10 @@
         for first in range(0, lanes, width):
             val = slice(first, first + width)
             tap = slice(lanes + first, lanes + first + width)
-            val_re = {i: spectra[i, re, val] for i in values}
-            val_im = {i: spectra[i, im, val] for i in values}
-            tap_re = {j: spectra[j, re, tap] for j in taps}
-            tap_im = {j: spectra[j, im, tap] for j in taps}
+            val_re = {i: at(i)[re, val] for i in values}
+            val_im = {i: at(i)[im, val] for i in values}
+            tap_re = {j: at(j)[re, tap] for j in taps}
+            tap_im = {j: at(j)[im, tap] for j in taps}
             if 0 in taps:
                 tap_re[0] = tap_re[0] + bias[:, pl.ds(base + first, width)]
             last_re = last_im = None
@@ -171,24 +173,25 @@
         @pl.when(missing == m)
         def _(m=m):
             products(
-                spectra, bias, sums, total, (), lambda i, j: m not in (i, j), lambda r: r < m
+                lambda i: spectra.at[i], spectra.shape, bias, sums, total, (), lambda i, j: m not in (i, j), lambda r: r < m
             )
             for r in range(m):
                 early[r] = inverse(total[r], back)
 
 
-def late_kernel(count, last, piece, bias, forward, back, sums, early, _, spectra, *refs):
-    outs, total, result = refs[:count], refs[count], refs[count + 1]
+def late_kernel(count, last, piece, bias, forward, back, sums, early, spectra, *refs):
+    outs, total, result, fresh = refs[:count], *refs[count:]
     me = lax.axis_index("ctx")
     missing = came(OUT, count, me, last)
-    transform_into(OUT, last, piece, forward, spectra)
+    x = piece[...]
+    fresh[0] = dot(forward[...], jnp.concatenate([x, x], 0))
     for m in range(count):
 
         @pl.when(missing == m)
         def _(m=m):
             ready = [r for r in range(count) if any(m not in (i, r - i) for i in range(r + 1))]
             products(
-                spectra, bias, sums, total, ready, lambda i, j: m in (i, j), lambda r: r >= m
+                lambda i: fresh.at[0] if i == m else spectra.at[i], spectra.shape, bias, sums, total, ready, lambda i, j: m in (i, j), lambda r: r >= m
             )
             for r in range(count):
                 result[r] = early[r] if r < m else inverse(total[r], back)
@@ -197,11 +200,12 @@
         outs[place][...] = result[to(BACK, count, me, step)]
 
 
-def whole_kernel(count, last, piece, bias, forward, back, _, spectra, *refs):
-    outs, total, result = refs[:count], refs[count], refs[count + 1]
+def whole_kernel(count, last, piece, bias, forward, back, held, *refs):
+    outs, total, result, spectra = refs[:count], *refs[count:]
+    spectra[...] = held[...]
     me = lax.axis_index("ctx")
     transform_into(OUT, last, piece, forward, spectra)
-    products(spectra, bias, None, total, (), lambda i, j: True, lambda r: True)
+    products(lambda i: spectra.at[i], spectra.shape, bias, None, total, (), lambda i, j: True, lambda r: True)
     for r in range(count):
         result[r] = inverse(total[r], back)
     for place, step in enumerate([0] + steps(BACK, count)):
@@ -229,18 +233,17 @@
         )(bias, back, spectra)
     return pl.pallas_call(
         functools.partial(late_kernel if held else whole_kernel, count, last),
-        out_shape=[jax.ShapeDtypeStruct(spectra.shape, jnp.float32)]
-        + [jax.ShapeDtypeStruct((rows, lanes), jnp.bfloat16)] * count,
+        out_shape=[jax.ShapeDtypeStruct((rows, lanes), jnp.bfloat16)] * count,
         in_specs=[VMEM] * (5 + len(held)),
-        out_specs=[VMEM] * (count + 1),
+        out_specs=[VMEM] * count,
         scratch_shapes=[
             pltpu.VMEM(totals.shape, totals.dtype),
             pltpu.VMEM(results.shape, results.dtype),
+            pltpu.VMEM((1 if held else count, length, both), jnp.float32),
         ],
-        input_output_aliases={4 + len(held): 0},
         compiler_params=pltpu.CompilerParams(vmem_limit_bytes=8 * MIB),
         name="convolve",
-    )(piece, bias, forward, back, *held, spectra)[1:]
+    )(piece, bias, forward, back, *held, spectra)
 
 
 def gated(gate, cols, piece):

time: 25.9 us -> 25.9 us (level)
  waiting for transfers between devices: 9.21 us -> 8.67 us
  Pallas kernels: 4.16 us -> 4.43 us
    ppermute x6, waiting for transfers between devices: 9.21 us -> 8.67 us  [move(): return lax.ppermute(piece, 'ctx', pairs(plan, count, step))]
    ppermute x6, starting transfers between devices: 10.2 us -> 10.4 us  [move(): return lax.ppermute(piece, 'ctx', pairs(plan, count, step))]
    pallas_call x3, Pallas kernels: 0.66 us -> 0.93 us  [transform(): pl.pallas_call(functools.partial(transform_kernel, step), out_shape=shape...]
  transfers between devices with their start and end apart: 6 -> 6, of which waited for: 5 -> 5; matrix products, arithmetic and copies ran while one was open for 4% -> 4% of each run, Pallas kernels for 13% -> 14%
where the time goes in v4:
time: 25.9 us; the launch traced here: 25.7 us
  starting transfers between devices  10.4 us (40%)
  waiting for transfers between devices  8.67 us (33%)
  Pallas kernels  4.43 us (17%)
  local copies, waits for them, and re-layouts  1.97 us (8%)
    ppermute x6, starting transfers between devices, move(): return lax.ppermute(piece, 'ctx', pairs(plan, count, step))  10.4 us
    ppermute x6, waiting for transfers between devices, move(): return lax.ppermute(piece, 'ctx', pairs(plan, count, step))  8.67 us
    dynamic_slice x2, local copies, waits for them, and re-layouts, piece(): lax.dynamic_slice_in_dim(array, start, lanes, 1)  1.95 us
    pallas_call x1, Pallas kernels, first_block(): pl.pallas_call(functools.partial(first_block_kernel, count, lanes), out_s...  1.64 us
    pallas_call x3, Pallas kernels, transform(): pl.pallas_call(functools.partial(transform_kernel, step), out_shape=shape...  0.93 us
    pallas_call x1, Pallas kernels, convolve(): pl.pallas_call(functools.partial(late_kernel if held else whole_kernel, c...  0.7 us
    pallas_call x2, Pallas kernels, put(): pl.pallas_call(functools.partial(put_kernel, places, count), out_shape=ja...  0.68 us
  transfers between devices with their start and end apart: 6, of which 5 were waited for; matrix products, arithmetic and copies ran while one was open for 4% of the time, Pallas kernels for 14%

profile of v4, /device:TPU:0, one launch (start us, length us, event | category | flops | bytes accessed | tf_op | source)
XLA Modules:
  0.0 25.7 jit_solution(10481957354202840080)
XLA Ops:
  0.0 0.0 copy-start
  0.0 0.9 %constant_dynamic-slice_fusion.2 = (bf16[128,256]{1,0:T(8,128)(2,1)S(1)}, bf16[128,256]{1,0:T(8,128)(2,1)S(1)}) fusion(bf16[128,4096]{1,0:T(8,128)(2,1)} %param.9, s32[]{:T(128)S(6)} %select_n.18, bf16[128,4096]{1,0:T(8,128)(2,1)} %param.6), kind=kLoop, calls=%fused_computation.6 | loop fusion | bytes 262148 | tf_op jit(solution)/shard_map/dynamic_slice | solution.py:70
  0.9 0.0 copy-start.1
  0.9 0.0 copy-start.2
  0.9 0.0 copy-start.3
  1.0 5.1 %collective-permute-start.2 = (bf16[128,512]{1,0:T(8,128)(2,1)S(1)}, bf16[128,512]{1,0:T(8,128)(2,1)S(1)}, u32[]{:S(2)}, u32[]{:S(2)}) collective-permute-start(bf16[128,512]{1,0:T(8,128)(2,1)S(1)} %pad_maximum_fusion.2.refs_0_), channel_id=1, source_target_pairs={{0,24},{8,16},{16,8},{24,0},{1,25},{9,17},{17,9},{25,1},{2,26},{10... | collective-permute-start | bytes 393224 | tf_op jit(solution)/shard_map/ppermute | solution.py:357
  6.1 1.0 %constant_dynamic-slice_fusion = (bf16[128,256]{1,0:T(8,128)(2,1)S(1)}, bf16[128,256]{1,0:T(8,128)(2,1)S(1)}, bf16[128,256]{1,0:T(8,128)(2,1)S(1)}, bf16[128,256...) fusion(bf16[128,4096]{1,0:T(8,128)(2,1)} %param.9, s32[]{:T(128)S(6)} %select_n.19, ...), kind=kLoop, calls=%fused_computation.4 | loop fusion | bytes 786444 | tf_op jit(solution)/shard_map/dynamic_slice | solution.py:70
  7.1 0.1 collective-permute-start
  7.2 0.7 %collective-permute-start.1 = (bf16[128,512]{1,0:T(8,128)(2,1)S(1)}, bf16[128,512]{1,0:T(8,128)(2,1)S(1)}, u32[]{:S(2)}, u32[]{:S(2)}) collective-permute-start(bf16[128,512]{1,0:T(8,128)(2,1)S(1)} %pad_maximum_fusion.1.refs_1_), channel_id=1, source_target_pairs={{0,8},{8,0},{16,24},{24,16},{1,9},{9,1},{17,25},{25,17},{2,10},{10... | collective-permute-start | bytes 393224 | tf_op jit(solution)/shard_map/ppermute | solution.py:357
  7.9 0.0 copy-done
  7.9 0.2 transform.3.refs_2_
  8.2 0.0 copy-done.1
  8.2 0.0 copy-done.2
  8.2 0.0 copy-done.3
  8.2 1.6 %first_block.1 = (bf16[128,1024]{1,0:T(8,128)(2,1)}, f32[8,128]{1,0:T(8,128)S(1)}) custom-call(bf16[128,512]{1,0:T(8,128)(2,1)S(1)} %pad_maximum_fusion.2.refs_0_, bf16[128,512]{1,0:T(8,128)(2,1)S(1)} %pad_maximum_fusion.1.refs_1_, bf16[128,512]{1,0:T(8,128)(2,1)S(1)} %pad_maximum_fusion.refs_2_, f32[1,4096]{1,0:T(1,128)S(1)} %bitcast.1, ...), custom_call_target="tpu_custom_call" | custom-call | flops 201326592 | tf_op jit(solution)/shard_map/first_block/pallas_call | solution.py:283
  9.8 0.2 collective-permute-done.2.refs_0_
  10.0 0.4 %transform.4.refs_2_ = f32[4,256,512]{2,1,0:T(8,128)S(1)} custom-call(bf16[128,512]{1,0:T(8,128)(2,1)S(1)} %collective-permute-done.2.refs_0_, bf16[256,256]{1,0:T(8,128)(2,1)S(1)} %copy-done, f32[4,256,512]{2,1,0:T(8,128)S(1)} %transform.3.refs_2_, f32[8,128]{1,0:T(8,128)S(1)} %get-tuple-element.17.refs_3_), custom_call_target="tpu_custom_call", output_to_operand_aliasing={{}: (2, {})} | custom-call | flops 67108864 | bytes 524288 | tf_op jit(solution)/shard_map/transform/pallas_call | solution.py:95
  10.4 4.1 %collective-permute-done.1.refs_0_ = bf16[128,512]{1,0:T(8,128)(2,1)S(1)} collective-permute-done((bf16[128,512]{1,0:T(8,128)(2,1)S(1)}, bf16[128,512]{1,0:T(8,128)(2,1)S(1)}, u32[]{:S(2)}, u32[]{:S(2)}) %collective-permute-start.1) | collective-permute-done | bytes 131104 | tf_op jit(solution)/shard_map/ppermute | solution.py:357
  14.5 0.4 %transform.5.spectra = f32[4,256,512]{2,1,0:T(8,128)S(1)} custom-call(bf16[128,512]{1,0:T(8,128)(2,1)S(1)} %collective-permute-done.1.refs_0_, bf16[256,256]{1,0:T(8,128)(2,1)S(1)} %copy-done, f32[4,256,512]{2,1,0:T(8,128)S(1)} %transform.4.refs_2_), custom_call_target="tpu_custom_call", output_to_operand_aliasing={{}: (2, {})} | custom-call | flops 67108864 | bytes 524288 | tf_op jit(solution)/shard_map/transform/pallas_call | solution.py:95
  14.9 0.5 %early_products.1 = (f32[4,256,256]{2,1,0:T(8,128)S(1)}, bf16[4,128,256]{2,1,0:T(8,128)(2,1)S(1)}) custom-call(f32[1,4096]{1,0:T(1,128)S(1)} %bitcast.2, bf16[128,768]{1,0:T(8,128)(2,1)S(1)} %copy-done.2, f32[4,256,512]{2,1,0:T(8,128)S(1)} %transform.5.spectra), custom_call_target="tpu_custom_call" | custom-call | flops 150994944 | bytes 2097152 | tf_op jit(solution)/shard_map/early_products/pallas_call | solution.py:222
  15.4 1.8 %collective-permute-done.piece = bf16[128,512]{1,0:T(8,128)(2,1)S(1)} collective-permute-done((bf16[128,512]{1,0:T(8,128)(2,1)S(1)}, bf16[128,512]{1,0:T(8,128)(2,1)S(1)}, u32[]{:S(2)}, u32[]{:S(2)}) %collective-permute-start) | collective-permute-done | bytes 131104 | tf_op jit(solution)/shard_map/ppermute | solution.py:357
  17.2 0.7 %convolve.1 = (bf16[128,256]{1,0:T(8,128)(2,1)S(1)}, bf16[128,256]{1,0:T(8,128)(2,1)S(1)}, bf16[128,256]{1,0:T(8,128)(2,1)S(1)}, bf16[128,256]{1,0:T(8,128)(2,1)S(1)}) custom-call(bf16[128,512]{1,0:T(8,128)(2,1)S(1)} %collective-permute-done.piece, f32[1,4096]{1,0:T(1,128)S(1)} %bitcast.3, bf16[256,256]{1,0:T(8,128)(2,1)S(1)} %copy-done, ...), custom_call_target="tpu_custom_call" | custom-call | tf_op jit(solution)/shard_map/convolve/pallas_call | solution.py:234
  17.9 0.7 %collective-permute-start.3 = (bf16[128,256]{1,0:T(8,128)(2,1)S(1)}, bf16[128,256]{1,0:T(8,128)(2,1)S(1)}, u32[]{:S(2)}, u32[]{:S(2)}) collective-permute-start(bf16[128,256]{1,0:T(8,128)(2,1)S(1)} %get-tuple-element.20), channel_id=1, source_target_pairs={{0,16},{8,24},{16,0},{24,8},{1,17},{9,25},{17,1},{25,9},{2,18},{10... | collective-permute-start | bytes 196616 | tf_op jit(solution)/shard_map/ppermute | solution.py:357
  18.6 2.5 %collective-permute-start.4 = (bf16[128,256]{1,0:T(8,128)(2,1)S(1)}, bf16[128,256]{1,0:T(8,128)(2,1)S(1)}, u32[]{:S(2)}, u32[]{:S(2)}) collective-permute-start(bf16[128,256]{1,0:T(8,128)(2,1)S(1)} %get-tuple-element.21), channel_id=1, source_target_pairs={{0,8},{8,16},{16,24},{24,0},{1,9},{9,17},{17,25},{25,1},{2,10},{10... | collective-permute-start | bytes 196616 | tf_op jit(solution)/shard_map/ppermute | solution.py:357
  21.1 1.3 %collective-permute-start.5 = (bf16[128,256]{1,0:T(8,128)(2,1)S(1)}, bf16[128,256]{1,0:T(8,128)(2,1)S(1)}, u32[]{:S(2)}, u32[]{:S(2)}) collective-permute-start(bf16[128,256]{1,0:T(8,128)(2,1)S(1)} %get-tuple-element.22), channel_id=1, source_target_pairs={{0,24},{8,0},{16,8},{24,16},{1,25},{9,1},{17,9},{25,17},{2,26},{10... | collective-permute-start | bytes 196616 | tf_op jit(solution)/shard_map/ppermute | solution.py:357
  22.4 0.7 %put.2.refs_4_ = bf16[128,1024]{1,0:T(8,128)(2,1)} custom-call(bf16[128,256]{1,0:T(8,128)(2,1)S(1)} %get-tuple-element.23.refs_0_, bf16[128,1024]{1,0:T(8,128)(2,1)S(1)} %copy-done.1, bf16[128,1024]{1,0:T(8,128)(2,1)} %get-tuple-element.24.refs_2_), custom_call_target="tpu_custom_call", output_to_operand_aliasing={{}: (2, {})} | custom-call | tf_op jit(solution)/shard_map/put/pallas_call | solution.py:334
  23.1 2.2 %collective-permute-done.3.refs_0_ = bf16[128,256]{1,0:T(8,128)(2,1)S(1)} collective-permute-done((bf16[128,256]{1,0:T(8,128)(2,1)S(1)}, bf16[128,256]{1,0:T(8,128)(2,1)S(1)}, u32[]{:S(2)}, u32[]{:S(2)}) %collective-permute-start.3) | collective-permute-done | bytes 65568 | tf_op jit(solution)/shard_map/ppermute | solution.py:357
  25.3 0.0 collective-permute-done.4.refs_1_
  25.3 0.4 %collective-permute-done.5.refs_2_ = bf16[128,256]{1,0:T(8,128)(2,1)S(1)} collective-permute-done((bf16[128,256]{1,0:T(8,128)(2,1)S(1)}, bf16[128,256]{1,0:T(8,128)(2,1)S(1)}, u32[]{:S(2)}, u32[]{:S(2)}) %collective-permute-start.5) | collective-permute-done | bytes 65568 | tf_op jit(solution)/shard_map/ppermute | solution.py:357
  (5 shorter events, 0.1 us)
Async XLA Ops:
  0.0 7.9 %copy-start = (bf16[256,256]{1,0:T(8,128)(2,1)S(1)}, bf16[256,256]{1,0:T(8,128)(2,1)}, u32[]{:S(2)}) copy-start(bf16[256,256]{1,0:T(8,128)(2,1)} %constant.27.clone.refs_1_.refs_4_.forward) | copy-start | bytes 393220
  0.9 7.2 %copy-start.1 = (bf16[128,1024]{1,0:T(8,128)(2,1)S(1)}, bf16[128,1024]{1,0:T(8,128)(2,1)}, u32[]{:S(2)}) copy-start(bf16[128,1024]{1,0:T(8,128)(2,1)} %refs_3_.1) | copy-start | bytes 786436
  0.9 7.2 %copy-start.2 = (bf16[128,768]{1,0:T(8,128)(2,1)S(1)}, bf16[128,768]{1,0:T(8,128)(2,1)}, u32[]{:S(2)}) copy-start(bf16[128,768]{1,0:T(8,128)(2,1)} %constant.28.clone.refs_5_.back) | copy-start | bytes 589828
  0.9 7.2 %copy-start.3 = (f32[4096]{0:T(1024)S(1)}, f32[4096]{0:T(1024)}, u32[]{:S(2)}) copy-start(f32[4096]{0:T(1024)} %param.8) | copy-start | bytes 49156
  1.0 9.0 %collective-permute-start.2 = (bf16[128,512]{1,0:T(8,128)(2,1)S(1)}, bf16[128,512]{1,0:T(8,128)(2,1)S(1)}, u32[]{:S(2)}, u32[]{:S(2)}) collective-permute-start(bf16[128,512]{1,0:T(8,128)(2,1)S(1)} %pad_maximum_fusion.2.refs_0_), channel_id=1, source_target_pairs={{0,24},{8,16},{16,8},{24,0},{1,25},{9,17},{17,9},{25,1},{2,26},{10... | collective-permute-start | bytes 393224 | tf_op jit(solution)/shard_map/ppermute | solution.py:357
  7.1 10.0 %collective-permute-start = (bf16[128,512]{1,0:T(8,128)(2,1)S(1)}, bf16[128,512]{1,0:T(8,128)(2,1)S(1)}, u32[]{:S(2)}, u32[]{:S(2)}) collective-permute-start(bf16[128,512]{1,0:T(8,128)(2,1)S(1)} %pad_maximum_fusion.refs_2_), channel_id=1, source_target_pairs={{0,16},{8,24},{16,0},{24,8},{1,17},{9,25},{17,1},{25,9},{2,18},{10... | collective-permute-start | bytes 393224 | tf_op jit(solution)/shard_map/ppermute | solution.py:357
  7.2 7.3 %collective-permute-start.1 = (bf16[128,512]{1,0:T(8,128)(2,1)S(1)}, bf16[128,512]{1,0:T(8,128)(2,1)S(1)}, u32[]{:S(2)}, u32[]{:S(2)}) collective-permute-start(bf16[128,512]{1,0:T(8,128)(2,1)S(1)} %pad_maximum_fusion.1.refs_1_), channel_id=1, source_target_pairs={{0,8},{8,0},{16,24},{24,16},{1,9},{9,1},{17,25},{25,17},{2,10},{10... | collective-permute-start | bytes 393224 | tf_op jit(solution)/shard_map/ppermute | solution.py:357
  17.9 7.4 %collective-permute-start.3 = (bf16[128,256]{1,0:T(8,128)(2,1)S(1)}, bf16[128,256]{1,0:T(8,128)(2,1)S(1)}, u32[]{:S(2)}, u32[]{:S(2)}) collective-permute-start(bf16[128,256]{1,0:T(8,128)(2,1)S(1)} %get-tuple-element.20), channel_id=1, source_target_pairs={{0,16},{8,24},{16,0},{24,8},{1,17},{9,25},{17,1},{25,9},{2,18},{10... | collective-permute-start | bytes 196616 | tf_op jit(solution)/shard_map/ppermute | solution.py:357
  18.6 6.7 %collective-permute-start.4 = (bf16[128,256]{1,0:T(8,128)(2,1)S(1)}, bf16[128,256]{1,0:T(8,128)(2,1)S(1)}, u32[]{:S(2)}, u32[]{:S(2)}) collective-permute-start(bf16[128,256]{1,0:T(8,128)(2,1)S(1)} %get-tuple-element.21), channel_id=1, source_target_pairs={{0,8},{8,16},{16,24},{24,0},{1,9},{9,17},{17,25},{25,1},{2,10},{10... | collective-permute-start | bytes 196616 | tf_op jit(solution)/shard_map/ppermute | solution.py:357
  21.1 4.6 %collective-permute-start.5 = (bf16[128,256]{1,0:T(8,128)(2,1)S(1)}, bf16[128,256]{1,0:T(8,128)(2,1)S(1)}, u32[]{:S(2)}, u32[]{:S(2)}) collective-permute-start(bf16[128,256]{1,0:T(8,128)(2,1)S(1)} %get-tuple-element.22), channel_id=1, source_target_pairs={{0,24},{8,0},{16,8},{24,16},{1,25},{9,1},{17,9},{25,17},{2,26},{10... | collective-permute-start | bytes 196616 | tf_op jit(solution)/shard_map/ppermute | solution.py:357

commit v5 on v4

--- a/solution.py
+++ b/solution.py
@@ -13,7 +13,7 @@
 MIB = 1 << 20
 VMEM = pl.BlockSpec(memory_space=pltpu.VMEM)
 OUT = ("swap", 3, 1, 2)
-BACK = ("ring", 2, 1, 3)
+BACK = ("swap", 2, 3, 1)
 
 
 def split(table):

time: 25.9 us -> 25.9 us (level)
  waiting for transfers between devices: 8.67 us -> 9.74 us
  starting transfers between devices: 10.4 us -> 9.42 us
    ppermute x6, waiting for transfers between devices: 8.67 us -> 9.74 us  [move(): return lax.ppermute(piece, 'ctx', pairs(plan, count, step))]
    ppermute x6, starting transfers between devices: 10.4 us -> 9.42 us  [move(): return lax.ppermute(piece, 'ctx', pairs(plan, count, step))]
where the time goes in v5:
time: 25.9 us; the launch traced here: 25.8 us
  waiting for transfers between devices  9.74 us (38%)
  starting transfers between devices  9.42 us (36%)
  Pallas kernels  4.43 us (17%)
  local copies, waits for them, and re-layouts  1.97 us (8%)
    ppermute x6, waiting for transfers between devices, move(): return lax.ppermute(piece, 'ctx', pairs(plan, count, step))  9.74 us
    ppermute x6, starting transfers between devices, move(): return lax.ppermute(piece, 'ctx', pairs(plan, count, step))  9.42 us
    dynamic_slice x2, local copies, waits for them, and re-layouts, piece(): lax.dynamic_slice_in_dim(array, start, lanes, 1)  1.95 us
    pallas_call x1, Pallas kernels, first_block(): pl.pallas_call(functools.partial(first_block_kernel, count, lanes), out_s...  1.64 us
    pallas_call x3, Pallas kernels, transform(): pl.pallas_call(functools.partial(transform_kernel, step), out_shape=shape...  0.93 us
    pallas_call x1, Pallas kernels, convolve(): pl.pallas_call(functools.partial(late_kernel if held else whole_kernel, c...  0.69 us
    pallas_call x2, Pallas kernels, put(): pl.pallas_call(functools.partial(put_kernel, places, count), out_shape=ja...  0.68 us
  transfers between devices with their start and end apart: 6, of which 5 were waited for; matrix products, arithmetic and copies ran while one was open for 4% of the time, Pallas kernels for 14%

profile of v5, /device:TPU:0, one launch (start us, length us, event | category | flops | bytes accessed | tf_op | source)
XLA Modules:
  0.0 25.8 jit_solution(1516687061344502060)
XLA Ops:
  0.0 0.0 copy-start
  0.0 0.9 %constant_dynamic-slice_fusion.2 = (bf16[128,256]{1,0:T(8,128)(2,1)S(1)}, bf16[128,256]{1,0:T(8,128)(2,1)S(1)}) fusion(bf16[128,4096]{1,0:T(8,128)(2,1)} %param.9, s32[]{:T(128)S(6)} %select_n.18, bf16[128,4096]{1,0:T(8,128)(2,1)} %param.6), kind=kLoop, calls=%fused_computation.6 | loop fusion | bytes 262148 | tf_op jit(solution)/shard_map/dynamic_slice | solution.py:70
  0.9 0.0 copy-start.1
  0.9 0.0 copy-start.2
  0.9 0.0 copy-start.3
  1.0 5.1 %collective-permute-start.2 = (bf16[128,512]{1,0:T(8,128)(2,1)S(1)}, bf16[128,512]{1,0:T(8,128)(2,1)S(1)}, u32[]{:S(2)}, u32[]{:S(2)}) collective-permute-start(bf16[128,512]{1,0:T(8,128)(2,1)S(1)} %pad_maximum_fusion.2.refs_0_), channel_id=1, source_target_pairs={{0,24},{8,16},{16,8},{24,0},{1,25},{9,17},{17,9},{25,1},{2,26},{10... | collective-permute-start | bytes 393224 | tf_op jit(solution)/shard_map/ppermute | solution.py:357
  6.1 1.0 %constant_dynamic-slice_fusion = (bf16[128,256]{1,0:T(8,128)(2,1)S(1)}, bf16[128,256]{1,0:T(8,128)(2,1)S(1)}, bf16[128,256]{1,0:T(8,128)(2,1)S(1)}, bf16[128,256...) fusion(bf16[128,4096]{1,0:T(8,128)(2,1)} %param.9, s32[]{:T(128)S(6)} %select_n.19, ...), kind=kLoop, calls=%fused_computation.4 | loop fusion | bytes 786444 | tf_op jit(solution)/shard_map/dynamic_slice | solution.py:70
  7.1 0.1 collective-permute-start
  7.2 0.7 %collective-permute-start.1 = (bf16[128,512]{1,0:T(8,128)(2,1)S(1)}, bf16[128,512]{1,0:T(8,128)(2,1)S(1)}, u32[]{:S(2)}, u32[]{:S(2)}) collective-permute-start(bf16[128,512]{1,0:T(8,128)(2,1)S(1)} %pad_maximum_fusion.1.refs_1_), channel_id=1, source_target_pairs={{0,8},{8,0},{16,24},{24,16},{1,9},{9,1},{17,25},{25,17},{2,10},{10... | collective-permute-start | bytes 393224 | tf_op jit(solution)/shard_map/ppermute | solution.py:357
  7.9 0.0 copy-done
  7.9 0.2 transform.3.refs_2_
  8.2 0.0 copy-done.1
  8.2 0.0 copy-done.2
  8.2 0.0 copy-done.3
  8.2 1.6 %first_block.1 = (bf16[128,1024]{1,0:T(8,128)(2,1)}, f32[8,128]{1,0:T(8,128)S(1)}) custom-call(bf16[128,512]{1,0:T(8,128)(2,1)S(1)} %pad_maximum_fusion.2.refs_0_, bf16[128,512]{1,0:T(8,128)(2,1)S(1)} %pad_maximum_fusion.1.refs_1_, bf16[128,512]{1,0:T(8,128)(2,1)S(1)} %pad_maximum_fusion.refs_2_, f32[1,4096]{1,0:T(1,128)S(1)} %bitcast.1, ...), custom_call_target="tpu_custom_call" | custom-call | flops 201326592 | tf_op jit(solution)/shard_map/first_block/pallas_call | solution.py:283
  9.8 0.2 collective-permute-done.2.refs_0_
  10.0 0.4 %transform.4.refs_2_ = f32[4,256,512]{2,1,0:T(8,128)S(1)} custom-call(bf16[128,512]{1,0:T(8,128)(2,1)S(1)} %collective-permute-done.2.refs_0_, bf16[256,256]{1,0:T(8,128)(2,1)S(1)} %copy-done, f32[4,256,512]{2,1,0:T(8,128)S(1)} %transform.3.refs_2_, f32[8,128]{1,0:T(8,128)S(1)} %get-tuple-element.17.refs_3_), custom_call_target="tpu_custom_call", output_to_operand_aliasing={{}: (2, {})} | custom-call | flops 67108864 | bytes 524288 | tf_op jit(solution)/shard_map/transform/pallas_call | solution.py:95
  10.4 4.1 %collective-permute-done.1.refs_0_ = bf16[128,512]{1,0:T(8,128)(2,1)S(1)} collective-permute-done((bf16[128,512]{1,0:T(8,128)(2,1)S(1)}, bf16[128,512]{1,0:T(8,128)(2,1)S(1)}, u32[]{:S(2)}, u32[]{:S(2)}) %collective-permute-start.1) | collective-permute-done | bytes 131104 | tf_op jit(solution)/shard_map/ppermute | solution.py:357
  14.5 0.4 %transform.5.spectra = f32[4,256,512]{2,1,0:T(8,128)S(1)} custom-call(bf16[128,512]{1,0:T(8,128)(2,1)S(1)} %collective-permute-done.1.refs_0_, bf16[256,256]{1,0:T(8,128)(2,1)S(1)} %copy-done, f32[4,256,512]{2,1,0:T(8,128)S(1)} %transform.4.refs_2_), custom_call_target="tpu_custom_call", output_to_operand_aliasing={{}: (2, {})} | custom-call | flops 67108864 | bytes 524288 | tf_op jit(solution)/shard_map/transform/pallas_call | solution.py:95
  14.9 0.5 %early_products.1 = (f32[4,256,256]{2,1,0:T(8,128)S(1)}, bf16[4,128,256]{2,1,0:T(8,128)(2,1)S(1)}) custom-call(f32[1,4096]{1,0:T(1,128)S(1)} %bitcast.2, bf16[128,768]{1,0:T(8,128)(2,1)S(1)} %copy-done.2, f32[4,256,512]{2,1,0:T(8,128)S(1)} %transform.5.spectra), custom_call_target="tpu_custom_call" | custom-call | flops 150994944 | bytes 2097152 | tf_op jit(solution)/shard_map/early_products/pallas_call | solution.py:222
  15.4 1.8 %collective-permute-done.piece = bf16[128,512]{1,0:T(8,128)(2,1)S(1)} collective-permute-done((bf16[128,512]{1,0:T(8,128)(2,1)S(1)}, bf16[128,512]{1,0:T(8,128)(2,1)S(1)}, u32[]{:S(2)}, u32[]{:S(2)}) %collective-permute-start) | collective-permute-done | bytes 131104 | tf_op jit(solution)/shard_map/ppermute | solution.py:357
  17.2 0.7 %convolve.1 = (bf16[128,256]{1,0:T(8,128)(2,1)S(1)}, bf16[128,256]{1,0:T(8,128)(2,1)S(1)}, bf16[128,256]{1,0:T(8,128)(2,1)S(1)}, bf16[128,256]{1,0:T(8,128)(2,1)S(1)}) custom-call(bf16[128,512]{1,0:T(8,128)(2,1)S(1)} %collective-permute-done.piece, f32[1,4096]{1,0:T(1,128)S(1)} %bitcast.3, bf16[256,256]{1,0:T(8,128)(2,1)S(1)} %copy-done, ...), custom_call_target="tpu_custom_call" | custom-call | tf_op jit(solution)/shard_map/convolve/pallas_call | solution.py:234
  17.9 0.7 %collective-permute-start.3 = (bf16[128,256]{1,0:T(8,128)(2,1)S(1)}, bf16[128,256]{1,0:T(8,128)(2,1)S(1)}, u32[]{:S(2)}, u32[]{:S(2)}) collective-permute-start(bf16[128,256]{1,0:T(8,128)(2,1)S(1)} %get-tuple-element.20), channel_id=1, source_target_pairs={{0,16},{8,24},{16,0},{24,8},{1,17},{9,25},{17,1},{25,9},{2,18},{10... | collective-permute-start | bytes 196616 | tf_op jit(solution)/shard_map/ppermute | solution.py:357
  18.6 2.4 %collective-permute-start.4 = (bf16[128,256]{1,0:T(8,128)(2,1)S(1)}, bf16[128,256]{1,0:T(8,128)(2,1)S(1)}, u32[]{:S(2)}, u32[]{:S(2)}) collective-permute-start(bf16[128,256]{1,0:T(8,128)(2,1)S(1)} %get-tuple-element.21), channel_id=1, source_target_pairs={{0,24},{8,16},{16,8},{24,0},{1,25},{9,17},{17,9},{25,1},{2,26},{10... | collective-permute-start | bytes 196616 | tf_op jit(solution)/shard_map/ppermute | solution.py:357
  21.0 0.4 %collective-permute-start.5 = (bf16[128,256]{1,0:T(8,128)(2,1)S(1)}, bf16[128,256]{1,0:T(8,128)(2,1)S(1)}, u32[]{:S(2)}, u32[]{:S(2)}) collective-permute-start(bf16[128,256]{1,0:T(8,128)(2,1)S(1)} %get-tuple-element.22), channel_id=1, source_target_pairs={{0,8},{8,0},{16,24},{24,16},{1,9},{9,1},{17,25},{25,17},{2,10},{10... | collective-permute-start | bytes 196616 | tf_op jit(solution)/shard_map/ppermute | solution.py:357
  21.4 0.7 %put.2.refs_4_ = bf16[128,1024]{1,0:T(8,128)(2,1)} custom-call(bf16[128,256]{1,0:T(8,128)(2,1)S(1)} %get-tuple-element.23.refs_0_, bf16[128,1024]{1,0:T(8,128)(2,1)S(1)} %copy-done.1, bf16[128,1024]{1,0:T(8,128)(2,1)} %get-tuple-element.24.refs_2_), custom_call_target="tpu_custom_call", output_to_operand_aliasing={{}: (2, {})} | custom-call | tf_op jit(solution)/shard_map/put/pallas_call | solution.py:334
  22.1 3.2 %collective-permute-done.3.refs_0_ = bf16[128,256]{1,0:T(8,128)(2,1)S(1)} collective-permute-done((bf16[128,256]{1,0:T(8,128)(2,1)S(1)}, bf16[128,256]{1,0:T(8,128)(2,1)S(1)}, u32[]{:S(2)}, u32[]{:S(2)}) %collective-permute-start.3) | collective-permute-done | bytes 65568 | tf_op jit(solution)/shard_map/ppermute | solution.py:357
  25.3 0.0 collective-permute-done.4.refs_1_
  25.3 0.5 %collective-permute-done.5.refs_2_ = bf16[128,256]{1,0:T(8,128)(2,1)S(1)} collective-permute-done((bf16[128,256]{1,0:T(8,128)(2,1)S(1)}, bf16[128,256]{1,0:T(8,128)(2,1)S(1)}, u32[]{:S(2)}, u32[]{:S(2)}) %collective-permute-start.5) | collective-permute-done | bytes 65568 | tf_op jit(solution)/shard_map/ppermute | solution.py:357
  (5 shorter events, 0.1 us)
Async XLA Ops:
  0.0 7.9 %copy-start = (bf16[256,256]{1,0:T(8,128)(2,1)S(1)}, bf16[256,256]{1,0:T(8,128)(2,1)}, u32[]{:S(2)}) copy-start(bf16[256,256]{1,0:T(8,128)(2,1)} %constant.27.clone.refs_1_.refs_4_.forward) | copy-start | bytes 393220
  0.9 7.2 %copy-start.1 = (bf16[128,1024]{1,0:T(8,128)(2,1)S(1)}, bf16[128,1024]{1,0:T(8,128)(2,1)}, u32[]{:S(2)}) copy-start(bf16[128,1024]{1,0:T(8,128)(2,1)} %refs_3_.1) | copy-start | bytes 786436
  0.9 7.2 %copy-start.2 = (bf16[128,768]{1,0:T(8,128)(2,1)S(1)}, bf16[128,768]{1,0:T(8,128)(2,1)}, u32[]{:S(2)}) copy-start(bf16[128,768]{1,0:T(8,128)(2,1)} %constant.28.clone.refs_5_.back) | copy-start | bytes 589828
  0.9 7.2 %copy-start.3 = (f32[4096]{0:T(1024)S(1)}, f32[4096]{0:T(1024)}, u32[]{:S(2)}) copy-start(f32[4096]{0:T(1024)} %param.8) | copy-start | bytes 49156
  1.0 9.0 %collective-permute-start.2 = (bf16[128,512]{1,0:T(8,128)(2,1)S(1)}, bf16[128,512]{1,0:T(8,128)(2,1)S(1)}, u32[]{:S(2)}, u32[]{:S(2)}) collective-permute-start(bf16[128,512]{1,0:T(8,128)(2,1)S(1)} %pad_maximum_fusion.2.refs_0_), channel_id=1, source_target_pairs={{0,24},{8,16},{16,8},{24,0},{1,25},{9,17},{17,9},{25,1},{2,26},{10... | collective-permute-start | bytes 393224 | tf_op jit(solution)/shard_map/ppermute | solution.py:357
  7.1 10.0 %collective-permute-start = (bf16[128,512]{1,0:T(8,128)(2,1)S(1)}, bf16[128,512]{1,0:T(8,128)(2,1)S(1)}, u32[]{:S(2)}, u32[]{:S(2)}) collective-permute-start(bf16[128,512]{1,0:T(8,128)(2,1)S(1)} %pad_maximum_fusion.refs_2_), channel_id=1, source_target_pairs={{0,16},{8,24},{16,0},{24,8},{1,17},{9,25},{17,1},{25,9},{2,18},{10... | collective-permute-start | bytes 393224 | tf_op jit(solution)/shard_map/ppermute | solution.py:357
  7.2 7.3 %collective-permute-start.1 = (bf16[128,512]{1,0:T(8,128)(2,1)S(1)}, bf16[128,512]{1,0:T(8,128)(2,1)S(1)}, u32[]{:S(2)}, u32[]{:S(2)}) collective-permute-start(bf16[128,512]{1,0:T(8,128)(2,1)S(1)} %pad_maximum_fusion.1.refs_1_), channel_id=1, source_target_pairs={{0,8},{8,0},{16,24},{24,16},{1,9},{9,1},{17,25},{25,17},{2,10},{10... | collective-permute-start | bytes 393224 | tf_op jit(solution)/shard_map/ppermute | solution.py:357
  17.9 7.4 %collective-permute-start.3 = (bf16[128,256]{1,0:T(8,128)(2,1)S(1)}, bf16[128,256]{1,0:T(8,128)(2,1)S(1)}, u32[]{:S(2)}, u32[]{:S(2)}) collective-permute-start(bf16[128,256]{1,0:T(8,128)(2,1)S(1)} %get-tuple-element.20), channel_id=1, source_target_pairs={{0,16},{8,24},{16,0},{24,8},{1,17},{9,25},{17,1},{25,9},{2,18},{10... | collective-permute-start | bytes 196616 | tf_op jit(solution)/shard_map/ppermute | solution.py:357
  18.6 6.7 %collective-permute-start.4 = (bf16[128,256]{1,0:T(8,128)(2,1)S(1)}, bf16[128,256]{1,0:T(8,128)(2,1)S(1)}, u32[]{:S(2)}, u32[]{:S(2)}) collective-permute-start(bf16[128,256]{1,0:T(8,128)(2,1)S(1)} %get-tuple-element.21), channel_id=1, source_target_pairs={{0,24},{8,16},{16,8},{24,0},{1,25},{9,17},{17,9},{25,1},{2,26},{10... | collective-permute-start | bytes 196616 | tf_op jit(solution)/shard_map/ppermute | solution.py:357
  21.0 4.7 %collective-permute-start.5 = (bf16[128,256]{1,0:T(8,128)(2,1)S(1)}, bf16[128,256]{1,0:T(8,128)(2,1)S(1)}, u32[]{:S(2)}, u32[]{:S(2)}) collective-permute-start(bf16[128,256]{1,0:T(8,128)(2,1)S(1)} %get-tuple-element.22), channel_id=1, source_target_pairs={{0,8},{8,0},{16,24},{24,16},{1,9},{9,1},{17,25},{25,17},{2,10},{10... | collective-permute-start | bytes 196616 | tf_op jit(solution)/shard_map/ppermute | solution.py:357
